TPU v7x, 32 devices: a whole 2x2x4 slice. The times are simulated.
32 devices in a mesh: tok: 16 (over z, x, core), ch: 2 (over y).
Axes of the slice: x: 2, y: 2, z: 4, core: 2. Of those that a mesh axis runs over, the one named last changes fastest.
Arguments:
- tokens: bfloat16 [4096, 384], P(('tok', 'ch')), may hold values from -6 to 6
- cotangent: bfloat16 [4096, 384], P(('tok', 'ch')), may hold values from -6 to 6
- norm_gain: float32 [384], replicated, may hold values from 0.5 to 1.5
- in_proj: bfloat16 [384, 1536], replicated, may hold values from -0.3125 to 0.3125
- conv_weight: float32 [2, 4, 768], P(None, None, 'ch'), may hold values from -3 to 3
- conv_bias: float32 [2, 768], P(None, 'ch'), may hold values from -3 to 3
- select_proj: float32 [2, 768, 56], P(None, 'ch'), may hold values from -0.21875 to 0.21875
- step_proj: float32 [2, 24, 768], P(None, None, 'ch'), may hold values from -1.25 to 1.25
- step_bias: float32 [2, 768], P(None, 'ch'), may hold values from -5 to -2
- decay_log: float32 [2, 16, 768], P(None, None, 'ch'), may hold values from -5.3 to 0.7
- skip_gain: float32 [2, 768], P(None, 'ch'), may hold values from 0.5 to 1.5
- out_proj: bfloat16 [768, 384], P('ch'), may hold values from -0.4375 to 0.4375
- clip_lengths: int32 [16, 3], P('tok'), may hold values from 1 to 128, 256 in all within a row
Outputs:
- block_out: bfloat16 [4096, 384], P(('tok', 'ch'))
- grad_tokens: float32 [4096, 384], P(('tok', 'ch'))
- grad_gain: float32 [384], replicated
- grad_in_proj: float32 [384, 1536], replicated
- grad_conv_weight: float32 [2, 4, 768], P(None, None, 'ch')
- grad_conv_bias: float32 [2, 768], P(None, 'ch')
- grad_select_proj: float32 [2, 768, 56], P(None, 'ch')
- grad_step_proj: float32 [2, 24, 768], P(None, None, 'ch')
- grad_step_bias: float32 [2, 768], P(None, 'ch')
- grad_decay_log: float32 [2, 16, 768], P(None, None, 'ch')
- grad_skip_gain: float32 [2, 768], P(None, 'ch')
- grad_out_proj: float32 [768, 384], P('ch')
Inputs may be any that keep to these rules, and one draw needn't show every extreme that they name: `clip_lengths`: each row gives the lengths of the 3 clips packed in order into one group of 256 tokens; a row sums to 256 and its longest clip has exactly 128 tokens.
All inputs are finite; a program needn't handle non-finite values.
Results may differ from a plain program's by a relative error of at most 0.01.
Values may be sent and summed in bfloat16 or wider, within the bound.
No kernel may reach another device: no remote copies, remote signals or barrier semaphores. Data moves between devices by JAX's collectives and lax.ppermute only.
A program may use at most 128 MiB of HBM per device.

v0:
```python
import jax
import jax.numpy as jnp
from jax import lax
from jax.sharding import PartitionSpec as P

norm_eps = 1e-05


def shift_rows(values, offset, fill_value):
    if offset == 0:
        return values
    filler = jnp.full((abs(offset),) + values.shape[1:], fill_value, values.dtype)
    if offset > 0:
        return jnp.concatenate([filler, values[:-offset]], axis=0)
    return jnp.concatenate([values[-offset:], filler], axis=0)


def clip_masks(lengths, length_total):
    clip_ends = jnp.cumsum(lengths)
    clip_starts = clip_ends - lengths
    position = jnp.arange(length_total, dtype=jnp.int32)
    starts_here = jnp.any(position[:, None] == clip_starts[None, :], axis=1)
    ends_here = jnp.any(position[:, None] == (clip_ends - 1)[None, :], axis=1)
    member = jnp.sum((position[:, None] >= clip_ends[None, :]).astype(jnp.int32), axis=1)
    return (starts_here, ends_here, member)


def conv_silu(signal, conv_weight, conv_bias, member, direction_sign):
    tap_count = conv_weight.shape[0]
    summed = conv_bias[None, :] + jnp.zeros_like(signal)
    for lagged in range(tap_count):
        shifted = shift_rows(signal, direction_sign * lagged, 0.0)
        in_clip = shift_rows(member, direction_sign * lagged, -1) == member
        summed = summed + conv_weight[tap_count - 1 - lagged][None, :] * jnp.where(
            in_clip[:, None], shifted, 0.0
        )
    return jax.nn.silu(summed)


def blocked_states(step_size, activated, input_map, output_map, rates, resets, reverse):
    row_total, width = step_size.shape
    state_size = rates.shape[0]
    block_rows = 32
    block_count = row_total // block_rows
    keep_rows = 1.0 - resets.astype(jnp.float32)
    items = (
        step_size.reshape(block_count, block_rows, width),
        activated.reshape(block_count, block_rows, width),
        input_map.reshape(block_count, block_rows, state_size),
        output_map.reshape(block_count, block_rows, state_size),
        keep_rows.reshape(block_count, block_rows),
    )

    def run_block(carry, pieces):
        step_rows, active_rows, input_rows, output_rows, keep_block = pieces
        results = [None] * block_rows
        order = range(block_rows - 1, -1, -1) if reverse else range(block_rows)
        for row in order:
            decay = jnp.exp(step_rows[row][None, :] * rates) * keep_block[row]
            carry = (
                decay * carry
                + (step_rows[row] * active_rows[row])[None, :] * input_rows[row][:, None]
            )
            results[row] = jnp.sum(carry * output_rows[row][:, None], axis=0)
        return (carry, jnp.stack(results))

    start = jnp.zeros((state_size, width), jnp.float32)
    _, outputs = lax.scan(jax.checkpoint(run_block), start, items, reverse=reverse)
    return outputs.reshape(row_total, width)


def selective(activated, selected, step_proj, step_bias, decay_log, skip_gain, resets, reverse):
    rank_width = step_proj.shape[0]
    state_size = decay_log.shape[0]
    low_rank = selected[:, :rank_width]
    input_map = selected[:, rank_width : rank_width + state_size]
    output_map = selected[:, rank_width + state_size :]
    step_size = jax.nn.softplus(
        jnp.dot(low_rank, step_proj, precision=lax.Precision.HIGHEST) + step_bias[None, :]
    )
    rates = -jnp.exp(decay_log)
    scanned = blocked_states(step_size, activated, input_map, output_map, rates, resets, reverse)
    return scanned + skip_gain[None, :] * activated


def front_section(signal, conv_weight, conv_bias, select_proj, member, direction_sign):
    activated = conv_silu(signal, conv_weight, conv_bias, member, direction_sign)
    return (activated, jnp.dot(activated, select_proj, precision=lax.Precision.HIGHEST))


def rows_product(left_side, right_side):
    return lax.dot_general(
        left_side, right_side, (((0,), (0,)), ((), ())), preferred_element_type=jnp.float32
    )


def times_transposed(left_side, right_side):
    return lax.dot_general(
        left_side, right_side, (((1,), (1,)), ((), ())), preferred_element_type=jnp.float32
    )


def norm_piece(tokens_f, norm_gain):
    scale_row = lax.rsqrt(jnp.mean(tokens_f * tokens_f, axis=1, keepdims=True) + norm_eps)
    return tokens_f * scale_row * norm_gain[None, :]


def finish_gate(ahead, behind, gate_part):
    return (ahead + behind) * jax.nn.silu(gate_part) * 0.5


def stack_pair(first_grads, second_grads, slot_index):
    return jnp.stack([first_grads[slot_index], second_grads[slot_index]])


def local(
    tokens,
    cotangent,
    norm_gain,
    in_proj,
    conv_weight,
    conv_bias,
    select_proj,
    step_proj,
    step_bias,
    decay_log,
    skip_gain,
    out_proj,
    clip_lengths,
):
    row_count = tokens.shape[0]
    tokens_f = tokens.astype(jnp.float32)
    normed, norm_pull = jax.vjp(norm_piece, tokens_f, norm_gain)
    normed_low = normed.astype(jnp.bfloat16)
    projected = jnp.dot(normed_low, in_proj, preferred_element_type=jnp.float32).astype(
        jnp.bfloat16
    )
    projected = projected.reshape(row_count, 2, -1)
    channel_side = lax.all_to_all(projected, "ch", split_axis=2, concat_axis=0, tiled=True)
    signal = channel_side[:, 0, :].astype(jnp.float32)
    gate_part = channel_side[:, 1, :].astype(jnp.float32)
    starts_here, ends_here, member = clip_masks(clip_lengths[0], signal.shape[0])

    def front_ahead(signal_in, weight_in, offset_in, select_in):
        return front_section(signal_in, weight_in, offset_in, select_in, member, 1)

    def front_behind(signal_in, weight_in, offset_in, select_in):
        return front_section(signal_in, weight_in, offset_in, select_in, member, -1)

    def scan_ahead(activated, selected, proj_in, offset_in, log_in, skip_in):
        return selective(
            activated, selected, proj_in, offset_in, log_in, skip_in, starts_here, False
        )

    def scan_behind(activated, selected, proj_in, offset_in, log_in, skip_in):
        return selective(activated, selected, proj_in, offset_in, log_in, skip_in, ends_here, True)

    active_ahead, part_ahead = front_ahead(signal, conv_weight[0], conv_bias[0], select_proj[0])
    active_behind, part_behind = front_behind(signal, conv_weight[1], conv_bias[1], select_proj[1])
    picked_ahead, picked_behind = lax.psum((part_ahead, part_behind), "ch")
    out_ahead, pull_scan_ahead = jax.vjp(
        scan_ahead,
        active_ahead,
        picked_ahead,
        step_proj[0],
        step_bias[0],
        decay_log[0],
        skip_gain[0],
    )
    out_behind, pull_scan_behind = jax.vjp(
        scan_behind,
        active_behind,
        picked_behind,
        step_proj[1],
        step_bias[1],
        decay_log[1],
        skip_gain[1],
    )
    gated_f, finish_pull = jax.vjp(finish_gate, out_ahead, out_behind, gate_part)
    gated = gated_f.astype(jnp.bfloat16)
    whole_out = lax.all_gather(out_proj, "ch", axis=0, tiled=True)
    token_side = lax.all_to_all(gated, "ch", split_axis=0, concat_axis=1, tiled=True)
    block_sum = jnp.dot(token_side, whole_out, preferred_element_type=jnp.float32)
    weight_terms = rows_product(token_side, cotangent)
    grad_out_local = lax.psum_scatter(weight_terms, "ch", scatter_dimension=0, tiled=True)
    grad_back = times_transposed(cotangent, whole_out).astype(jnp.bfloat16)
    grad_gated = lax.all_to_all(grad_back, "ch", split_axis=1, concat_axis=0, tiled=True).astype(
        jnp.float32
    )
    block_out = (tokens_f + block_sum).astype(jnp.bfloat16)
    grad_ahead, grad_behind, grad_gate = finish_pull(grad_gated)
    scan_grads_ahead = pull_scan_ahead(grad_ahead)
    scan_grads_behind = pull_scan_behind(grad_behind)
    picked_grad_ahead, picked_grad_behind = lax.psum(
        (scan_grads_ahead[1], scan_grads_behind[1]), "ch"
    )
    _, pull_front_ahead = jax.vjp(front_ahead, signal, conv_weight[0], conv_bias[0], select_proj[0])
    front_grads_ahead = pull_front_ahead((scan_grads_ahead[0], picked_grad_ahead))
    _, pull_front_behind = jax.vjp(
        front_behind, signal, conv_weight[1], conv_bias[1], select_proj[1]
    )
    front_grads_behind = pull_front_behind((scan_grads_behind[0], picked_grad_behind))
    grad_signal = front_grads_ahead[0] + front_grads_behind[0]
    grad_channels = jnp.stack([grad_signal, grad_gate], axis=1).astype(jnp.bfloat16)
    grad_token_side = lax.all_to_all(
        grad_channels, "ch", split_axis=0, concat_axis=2, tiled=True
    ).reshape(row_count, -1)
    grad_in_local = rows_product(normed_low, grad_token_side)
    grad_normed = times_transposed(grad_token_side, in_proj)
    grad_tokens_norm, grad_gain_local = norm_pull(grad_normed)
    grad_tokens = cotangent.astype(jnp.float32) + grad_tokens_norm
    grad_gain, grad_in_proj = lax.psum((grad_gain_local, grad_in_local), ("tok", "ch"))
    (
        grad_conv_weight,
        grad_conv_bias,
        grad_select_proj,
        grad_step_proj,
        grad_step_bias,
        grad_decay_log,
        grad_skip_gain,
        grad_out_proj,
    ) = lax.psum(
        (
            stack_pair(front_grads_ahead, front_grads_behind, 1),
            stack_pair(front_grads_ahead, front_grads_behind, 2),
            stack_pair(front_grads_ahead, front_grads_behind, 3),
            stack_pair(scan_grads_ahead, scan_grads_behind, 2),
            stack_pair(scan_grads_ahead, scan_grads_behind, 3),
            stack_pair(scan_grads_ahead, scan_grads_behind, 4),
            stack_pair(scan_grads_ahead, scan_grads_behind, 5),
            grad_out_local,
        ),
        "tok",
    )
    return (
        block_out,
        grad_tokens,
        grad_gain,
        grad_in_proj,
        grad_conv_weight,
        grad_conv_bias,
        grad_select_proj,
        grad_step_proj,
        grad_step_bias,
        grad_decay_log,
        grad_skip_gain,
        grad_out_proj,
    )


def solution(mesh):
    return jax.shard_map(
        local,
        mesh=mesh,
        in_specs=(
            P(("tok", "ch"), None),
            P(("tok", "ch"), None),
            P(),
            P(),
            P(None, None, "ch"),
            P(None, "ch"),
            P(None, "ch", None),
            P(None, None, "ch"),
            P(None, "ch"),
            P(None, None, "ch"),
            P(None, "ch"),
            P("ch", None),
            P("tok", None),
        ),
        out_specs=(
            P(("tok", "ch"), None),
            P(("tok", "ch"), None),
            P(),
            P(),
            P(None, None, "ch"),
            P(None, "ch"),
            P(None, "ch", None),
            P(None, None, "ch"),
            P(None, "ch"),
            P(None, None, "ch"),
            P(None, "ch"),
            P("ch", None),
        ),
        check_vma=False,
    )
```

profile of v0, /device:TPU:0, one launch (start us, length us, event | category | flops | bytes accessed | tf_op | source)
XLA Modules:
  0.0 2831.5 jit_solution(104283440402949934)
XLA Ops:
  76.8 336.2 %while.81 = (s32[]{:T(128)}, f32[16,384]{1,0:T(8,128)S(1)}, f32[8,32,384]{2,1,0:T(8,128)}, f32[8,16,384]{2,1,0:T(8,128)}, f32[8,32,384]{2,1,0:T(8,128)}, /*index...) while((s32[]{:T(128)}, f32[16,384]{1,0:T(8,128)S(1)}, ...), condition=%wide.region_74.76_spmd.clone, body=%wide.region_41.75_spmd.clone.sunk | while | flops 1634339 | bytes 1539068 | solution.py:68
  419.1 348.7 %while.80 = (s32[]{:T(128)}, f32[16,384]{1,0:T(8,128)S(1)}, f32[8,32,384]{2,1,0:T(8,128)}, f32[8,16,384]{2,1,0:T(8,128)}, f32[8,32,384]{2,1,0:T(8,128)}, /*index...) while((s32[]{:T(128)}, f32[16,384]{1,0:T(8,128)S(1)}, ...), condition=%wide.region_38.40_spmd.clone, body=%wide.region_5.39_spmd.clone.sunk | while | flops 1886242 | bytes 1983889 | solution.py:68
  429.4 21.1 multiply_reduce_fusion.452
  473.0 21.1 multiply_reduce_fusion.452
  516.6 21.1 multiply_reduce_fusion.452
  560.1 21.1 multiply_reduce_fusion.452
  603.8 21.1 multiply_reduce_fusion.452
  647.3 21.1 multiply_reduce_fusion.452
  690.9 21.1 multiply_reduce_fusion.452
  734.6 21.1 multiply_reduce_fusion.452
  770.6 814.1 %while.82 = (s32[]{:T(128)}, f32[16,384]{1,0:T(8,128)S(1)}, f32[16,384]{1,0:T(8,128)S(1)}, f32[8,32,384]{2,1,0:T(8,128)}, f32[8,32,384]{2,1,0:T(8,128)}, /*index...) while((s32[]{:T(128)}, f32[16,384]{1,0:T(8,128)S(1)}, ...), condition=%wide.region_204.206_spmd.clone, body=%wide.region_75.205_spmd.clone.sunk | while | flops 8189956 | bytes 5330964 | solution.py:68
  1587.7 815.2 %while.83 = (s32[]{:T(128)}, f32[16,384]{1,0:T(8,128)S(1)}, f32[16,384]{1,0:T(8,128)S(1)}, f32[8,32,384]{2,1,0:T(8,128)}, f32[8,32,384]{2,1,0:T(8,128)}, /*index...) while((s32[]{:T(128)}, f32[16,384]{1,0:T(8,128)S(1)}, ...), condition=%wide.region_335.337_spmd.clone, body=%wide.region_206.336_spmd.clone.sunk | while | flops 8189955 | bytes 5330944 | solution.py:68
  1664.7 20.8 select_add_fusion.5
  1766.6 20.8 select_add_fusion.5
  1868.5 20.8 select_add_fusion.5
  1970.4 20.8 select_add_fusion.5
  2072.3 20.8 select_add_fusion.5
  2174.2 20.8 select_add_fusion.5
  2276.1 20.8 select_add_fusion.5
  2378.0 20.8 select_add_fusion.5
  2490.0 39.4 %psum.102 = f32[384]{0:T(512)} all-reduce(f32[384]{0:T(512)S(1)} %get-tuple-element.1808), channel_id=1, replica_groups=mesh['tok'=16,'ch'=2] {'tok','ch'}, use_global_device_ids=true, to_apply=%region_339.341 | all-reduce | flops 384 | bytes 3072 | tf_op jit(solution)/shard_map/psum | solution.py:212
  2530.2 47.9 %all-reduce.362.cloned.1.call-done = (f32[2,4,384]{2,1,0:T(4,128)}, f32[2,384]{1,0:T(2,128)}, f32[2,384]{1,0:T(2,128)}, f32[2,16,384]{2,1,0:T(8,128)}, f32[2,384]{1,0:T(2,128)}) async-done(((f32[2,4,384]{2,1,0:T(4,128)}, f32[2,384]{1,0:T(2,128)}, f32[2,384]{1,0:T(2,128)}, f32[2,16,384]{2,1,0:T(8,128)}, f32[2,384]{1,0:T(2,128)}), (f32[2,4,384]{2,1,0:T(4,128)}, f32[2,384]{1,0:T(2,128)}, f32[2,384]{1,0:T(2,128)}, ...) | async-done | bytes 70672 | tf_op jit(solution)/shard_map/psum | solution.py:222
  2578.1 142.0 %all-reduce.360.cloned.1.call-done = f32[384,1536]{1,0:T(8,128)} async-done(((f32[384,1536]{1,0:T(8,128)}), f32[384,1536]{1,0:T(8,128)}) %all-reduce.360.cloned.1.call-update) | async-done | bytes 2359312 | tf_op jit(solution)/shard_map/psum | solution.py:212
  2720.1 96.1 %all-reduce.364.cloned.1.call-done = (f32[2,384,56]{1,2,0:T(8,128)}, f32[2,24,384]{2,1,0:T(8,128)}, f32[384,384]{1,0:T(8,128)}) async-done(((f32[2,384,56]{1,2,0:T(8,128)}, f32[2,24,384]{2,1,0:T(8,128)}, f32[384,384]{1,0:T(8,128)}), (f32[2,384,56]{1,2,0:T(8,128)}, f32[2,24,384]{2,1,0:T(8,128)}, f32[384,384]{1,0:T(8,128)})) %all-reduce.364.cloned.1.call-update) | async-done | bytes 835600 | tf_op jit(solution)/shard_map/psum | solution.py:222
  (3215 shorter events, 2141.4 us)
Async XLA Ops:
  20.2 13.3 all-to-all-start.2
  33.5 9.8 all-to-all-start
  37.0 34.9 %all-reduce.368.cloned.1.call-start = ((), (), s32[]{:S(2)}) async-start(), calls=%async_computation.10 | async-start | bytes 229376 | tf_op jit(solution)/shard_map/psum | solution.py:160
  43.7 2375.1 %copy-start.1 = (bf16[128,2,2,384]{3,0,2,1:T(8,128)(2,1)}, bf16[128,2,2,384]{3,0,2,1:T(8,128)(2,1)S(1)}, u32[]{:S(2)}) copy-start(bf16[128,2,2,384]{3,0,2,1:T(8,128)(2,1)S(1)} %copy.113) | copy-start | bytes 1179652
  50.2 2390.1 %all-reduce.366.cloned.1.call-start = ((), (), s32[]{:S(2)}) async-start(), calls=%async_computation.9 | async-start | bytes 229376 | tf_op jit(solution)/shard_map/psum | solution.py:194
  419.1 351.6 %copy-start.20 = (f32[16,384]{1,0:T(8,128)S(1)}, f32[16,384]{1,0:T(8,128)}, u32[]{:S(2)}) copy-start(f32[16,384]{1,0:T(8,128)} %custom-call.2) | copy-start | bytes 73732
  419.1 351.6 %copy-start.25 = (f32[16,384]{1,0:T(8,128)S(1)}, f32[16,384]{1,0:T(8,128)}, u32[]{:S(2)}) copy-start(f32[16,384]{1,0:T(8,128)} %custom-call.3) | copy-start | bytes 73732
  467.8 30.4 %copy-start.36 = (f32[16]{0:T(128)S(1)}, f32[16]{0:T(128)}, u32[]{:S(2)}) copy-start(f32[16]{0:T(128)} %get-tuple-element.4293) | copy-start | bytes 196 | tf_op jit(solution)/shard_map/jvp()/while
  467.8 30.4 %copy-start.37 = (f32[16]{0:T(128)S(1)}, f32[16]{0:T(128)}, u32[]{:S(2)}) copy-start(f32[16]{0:T(128)} %get-tuple-element.4298) | copy-start | bytes 196 | tf_op jit(solution)/shard_map/jvp()/while
  598.5 30.4 %copy-start.36 = (f32[16]{0:T(128)S(1)}, f32[16]{0:T(128)}, u32[]{:S(2)}) copy-start(f32[16]{0:T(128)} %get-tuple-element.4293) | copy-start | bytes 196 | tf_op jit(solution)/shard_map/jvp()/while
  598.5 30.4 %copy-start.37 = (f32[16]{0:T(128)S(1)}, f32[16]{0:T(128)}, u32[]{:S(2)}) copy-start(f32[16]{0:T(128)} %get-tuple-element.4298) | copy-start | bytes 196 | tf_op jit(solution)/shard_map/jvp()/while
  642.1 30.4 %copy-start.36 = (f32[16]{0:T(128)S(1)}, f32[16]{0:T(128)}, u32[]{:S(2)}) copy-start(f32[16]{0:T(128)} %get-tuple-element.4293) | copy-start | bytes 196 | tf_op jit(solution)/shard_map/jvp()/while
  642.1 30.4 %copy-start.37 = (f32[16]{0:T(128)S(1)}, f32[16]{0:T(128)}, u32[]{:S(2)}) copy-start(f32[16]{0:T(128)} %get-tuple-element.4298) | copy-start | bytes 196 | tf_op jit(solution)/shard_map/jvp()/while
  729.4 30.4 %copy-start.36 = (f32[16]{0:T(128)S(1)}, f32[16]{0:T(128)}, u32[]{:S(2)}) copy-start(f32[16]{0:T(128)} %get-tuple-element.4293) | copy-start | bytes 196 | tf_op jit(solution)/shard_map/jvp()/while
  770.6 817.0 %copy-start.19 = (f32[16,384]{1,0:T(8,128)S(1)}, f32[16,384]{1,0:T(8,128)}, u32[]{:S(2)}) copy-start(f32[16,384]{1,0:T(8,128)} %custom-call.4) | copy-start | bytes 73732
  770.6 817.0 %copy-start.24 = (f32[16,384]{1,0:T(8,128)S(1)}, f32[16,384]{1,0:T(8,128)}, u32[]{:S(2)}) copy-start(f32[16,384]{1,0:T(8,128)} %custom-call.5) | copy-start | bytes 73732
  2448.4 9.0 all-to-all-start.1
  2452.5 76.8 %reduce-scatter.2.cloned.1.call-start = ((), (), s32[]{:S(2)}) async-start(), calls=%async_computation.6 | async-start | bytes 1769472 | tf_op jit(solution)/shard_map/reduce_scatter | solution.py:185
  2464.4 14.7 all-to-all-start.3
  2468.0 110.0 %all-reduce.362.cloned.1.call-start = ((), (), s32[]{:S(2)}) async-start(), calls=%async_computation.7 | async-start | bytes 141312 | tf_op jit(solution)/shard_map/psum | solution.py:222
  2470.1 250.0 %all-reduce.360.cloned.1.call-start = ((), (), s32[]{:S(2)}) async-start(), calls=%async_computation.5 | async-start | bytes 4718592 | tf_op jit(solution)/shard_map/psum | solution.py:212
  2481.5 334.7 %all-reduce.364.cloned.1.call-start = ((), (), s32[]{:S(2)}) async-start(), calls=%async_computation.8 | async-start | bytes 1671168 | tf_op jit(solution)/shard_map/psum | solution.py:222
  2489.4 40.0 %copy-start.103 = (f32[128]{0:T(128)S(1)}, f32[128]{0:T(128)}, u32[]{:S(2)}) copy-start(f32[128]{0:T(128)} %copy-done.102) | copy-start | bytes 1540
  2489.4 40.0 %copy-start.18 = (bf16[128,384]{1,0:T(8,128)(2,1)S(1)}, bf16[128,384]{1,0:T(8,128)(2,1)}, u32[]{:S(2)}) copy-start(bf16[128,384]{1,0:T(8,128)(2,1)} %param.23) | copy-start | bytes 294916
  (171 other events, 2617.7 us)
Sparse Core Ops, SparseCore 0:
  50.4 21.5 all-reduce.367
  2419.0 21.3 all-reduce.365
  2459.9 25.9 reduce-scatter.1
  2491.5 86.4 all-reduce.361
  2584.0 136.0 all-reduce.359
  2724.8 91.3 all-reduce.363
where the time goes:
time: 2870 us; the launch traced here: 2830 us
  other arithmetic  2050 us (71%)
  waiting for transfers between devices  343 us (12%)
  local copies, waits for them, and re-layouts  316 us (11%)
  blocking collectives  50.4 us (2%)
    reduce_sum x400, other arithmetic, run_block(): results[row] = jnp.sum(carry * output_rows[row][:, None], axis=0)  1600 us
    add_any x16, other arithmetic, blocked_states(): lax.scan(jax.checkpoint(run_block), start, items, reverse=reverse)  332 us
    psum x2, waiting for transfers between devices, local(): lax.psum((stack_pair(front_grads_ahead, front_grads_behind, 1), stack_pai...  144 us
    psum x1, waiting for transfers between devices, local(): lax.psum((grad_gain_local, grad_in_local), ('tok', 'ch'))  142 us
    slice x112, local copies, waits for them, and re-layouts, run_block(): decay = jnp.exp(step_rows[row][None, :] * rates) * keep_block[row]  86.8 us
    squeeze x80, local copies, waits for them, and re-layouts, blocked_states(): lax.scan(jax.checkpoint(run_block), start, items, reverse=reverse)  60.4 us
  transfers between devices with their start and end apart: 10, of which 8 were waited for; matrix products, arithmetic and copies ran while one was open for 1% of the time, Pallas kernels for 0%

commit v1 on v0

v1 whole, which is shorter than its diff:
```python
import functools
import math

import jax
import jax.numpy as jnp
import numpy as np
from jax import lax
from jax.experimental import pallas as pl
from jax.experimental.pallas import tpu as pltpu
from jax.sharding import PartitionSpec as P

norm_eps = 1e-05
F32 = jnp.float32
LOW = jnp.bfloat16
LANES = 128
HUGE_STEP = 1e30
LOG2E = math.log2(math.e)
LN2 = math.log(2.0)
BLOCK = 64
PAIRS = 8
PIECES = 4
FETCHES = 8


def mm(a, b):
    return lax.dot_general(a, b, (((1,), (0,)), ((), ())), preferred_element_type=F32)


def mm_nt(a, b):
    return lax.dot_general(a, b, (((1,), (1,)), ((), ())), preferred_element_type=F32)


def mm_tn(a, b):
    return lax.dot_general(a, b, (((0,), (0,)), ((), ())), preferred_element_type=F32)


def split(x):
    high = x.astype(LOW)
    return high, (x - high.astype(F32)).astype(LOW)


def mm3(dot, a, b):
    a_high, a_low = split(a)
    b_high, b_low = split(b)
    return dot(a_high, b_high) + (dot(a_high, b_low) + dot(a_low, b_high))


def round_up(x, m):
    return -(-x // m) * m


def wide(ref, *lead):
    parts = [ref[lead + (i,)] for i in range(ref.shape[len(lead)])]
    return parts[0] if len(parts) == 1 else jnp.concatenate(parts, axis=-1)


def row_time(r, length):
    return (r & 7) * length + (r >> 3)


def clip_places(len_ref, total, shape):
    t = row_time(lax.broadcasted_iota(jnp.int32, shape, 0), total // 8)
    clips = len_ref.shape[1]
    ends = []
    acc = 0
    for c in range(clips):
        acc = acc + len_ref[0, c]
        ends.append(acc)
    start = jnp.zeros(shape, jnp.int32)
    end = jnp.full(shape, total, jnp.int32)
    for c in range(clips - 1):
        start = jnp.where(t >= ends[c], ends[c], start)
    for c in range(clips - 2, -1, -1):
        end = jnp.where(t < ends[c], ends[c], end)
    return t - start, end - 1 - t


def order_matrix(first, rows, first_token, tokens, total):
    r = lax.broadcasted_iota(jnp.int32, (rows, tokens), 0) + first
    t = lax.broadcasted_iota(jnp.int32, (rows, tokens), 1) + first_token
    return jnp.where(row_time(r, total // 8) == t, 1.0, 0.0).astype(LOW)


def take_tokens(first, rows, total):
    t = lax.broadcasted_iota(jnp.int32, (rows, total), 0) + first
    r = lax.broadcasted_iota(jnp.int32, (rows, total), 1)
    return jnp.where(row_time(r, total // 8) == t, 1.0, 0.0).astype(LOW)


def halo_fill(ext_ref, total, halo, sl):
    for q in range(halo // 8):
        tail = ext_ref[pl.ds(total + 8 * q, 8), sl]
        ext_ref[pl.ds(8 * q, 8), sl] = pltpu.roll(tail, 1, 0)
        head = ext_ref[pl.ds(halo + 8 * q, 8), sl]
        ext_ref[pl.ds(halo + total + 8 * q, 8), sl] = pltpu.roll(head, 7, 0)


def link_blocks(gain, added, toward_end):
    row = lax.broadcasted_iota(jnp.int32, gain.shape, 0)
    for k in (1, 2, 4):
        shift = k if toward_end else 8 - k
        inside = (row >= k) if toward_end else (row < 8 - k)
        added_near = jnp.where(inside, pltpu.roll(added, shift, 0), 0.0)
        gain_near = jnp.where(inside, pltpu.roll(gain, shift, 0), 1.0)
        added = added + gain * added_near
        gain = gain * gain_near
    if toward_end:
        return jnp.where(row >= 1, pltpu.roll(added, 1, 0), 0.0)
    return jnp.where(row < 7, pltpu.roll(added, 7, 0), 0.0)


def over_rows(total, body):
    def step(i, carry):
        body(pl.multiple_of(i * BLOCK, BLOCK))
        return carry

    lax.fori_loop(0, total // BLOCK, step, 0)


def over_pairs(length, body, init):
    def trip(i, carry):
        for q in range(PAIRS):
            carry = body(i * PAIRS + q, carry)
        return carry

    return lax.fori_loop(0, length // 2 // PAIRS, trip, init)


def tile(lt):
    return slice(lt * LANES, (lt + 1) * LANES)


def lane(n):
    return slice(n * LANES, (n + 1) * LANES)


def sigmoid(x):
    return 0.5 * jnp.tanh(0.5 * x) + 0.5


def fetch_all(sources, targets, sems):
    copies = [pltpu.make_async_copy(a, b, sems.at[i]) for i, (a, b) in enumerate(zip(sources, targets))]
    for copy in copies:
        copy.start()
    return copies


def weight_kernel(dims, select_hbm, taps_hbm, bias_hbm, packed_ref, select_ref, taps_ref, bias_ref, sems):
    taps, real = taps_ref.shape[1:]
    xd = select_ref.shape[1]
    for copy in fetch_all((select_hbm, taps_hbm, bias_hbm), (select_ref, taps_ref, bias_ref), sems):
        copy.wait()
    parts = [select_ref[0], select_ref[1], jnp.zeros((LANES - 2 * xd, real), F32)]
    packed_ref[0:LANES, 0:real] = jnp.concatenate(parts, axis=0).astype(LOW)
    parts = []
    for d in range(2):
        parts += [taps_ref[d], bias_ref[d:d + 1, :]]
    parts.append(jnp.zeros((16 - 2 * (taps + 1), real), F32))
    high, low = split(jnp.concatenate(parts, axis=0))
    packed_ref[LANES:LANES + 16, 0:real] = high
    packed_ref[LANES + 16:LANES + 32, 0:real] = low
    if real < packed_ref.shape[1]:
        packed_ref[:, real:] = jnp.zeros((LANES + 32, packed_ref.shape[1] - real), LOW)


def fetch_kernel(n, *refs):
    sources, targets, sems = refs[:n], refs[n + 1:2 * n + 1], refs[-1]
    rows = sources[0].shape[0] // FETCHES
    parts = [pl.ds(i * rows, rows) for i in range(FETCHES)]
    for copy in fetch_all(
        [sources[0].at[part, :] for part in parts] + list(sources[1:]),
        [targets[0].at[part, :] for part in parts] + list(targets[1:]), sems,
    ):
        copy.wait()


def norm_kernel(dims, len_hbm, own_ref, gain_ref, win_ref, *refs):
    n_ch, n_tok, rows, width, chans, inner, rank, states, taps = dims
    total = rows * n_ch
    toks = [own_ref, *refs[:n_ch - 1]]
    normed_ref, xp_ref, sigs_ref, gate_ref, pos_ref, rem_ref, len_ref, sem = refs[n_ch - 1:]
    me = lax.axis_index("ch")
    fetch = pltpu.make_async_copy(len_hbm, len_ref, sem)
    fetch.start()
    gain = gain_ref[...][None, :]
    for r0 in range(0, total, 256):
        rr = slice(r0, r0 + 256)
        xp = 0.0
        for k in range(n_ch):
            xp = xp + mm(order_matrix(r0, 256, lax.rem(me + k, n_ch) * rows, rows, total), toks[k][...])
        xp_ref[rr, :] = xp.astype(LOW)
        scale = lax.rsqrt(jnp.mean(xp * xp, axis=1, keepdims=True) + norm_eps)
        normed_ref[rr, :] = (xp * scale * gain).astype(LOW)
    normed = normed_ref[...]
    for k in range(n_ch):
        j = lax.rem(me + k, n_ch)
        sigs_ref[k] = mm(normed, win_ref[:, pl.ds(pl.multiple_of(j * chans, LANES), chans)]).astype(LOW)
    gate_ref[...] = mm(
        normed, win_ref[:, pl.ds(pl.multiple_of(inner + me * chans, LANES), chans)]
    ).astype(LOW)
    fetch.wait()
    pos, rem = clip_places(len_ref, total, (total, LANES))
    pos_ref[...] = pos
    rem_ref[...] = rem


def conv_silu(dims, k, sigs_ref, pack_ref, pos_ref, rem_ref, act_refs, dsil_refs, ext_ref):
    n_ch, n_tok, rows, width, chans, inner, rank, states, taps = dims
    total = rows * n_ch
    halo = 8 * (taps - 1)
    ext_ref[pl.ds(halo, total), :] = sigs_ref[k].astype(F32)
    halo_fill(ext_ref, total, halo, slice(None))
    conv = conv_rows_of(pack_ref, taps)

    def conv_rows(r0):
        pos_b = pos_ref[pl.ds(r0, BLOCK), :]
        rem_b = rem_ref[pl.ds(r0, BLOCK), :]
        for lt in range(chans // LANES):
            sl = tile(lt)
            for d in range(2):
                inside = rem_b if d else pos_b
                at = d * (taps + 1)
                summed = conv[at + taps:at + taps + 1, sl] + conv[at + taps - 1:at + taps, sl] * ext_ref[
                    pl.ds(r0 + halo, BLOCK), sl
                ]
                for lag in range(1, taps):
                    far = ext_ref[pl.ds(r0 + (halo + 8 * lag if d else halo - 8 * lag), BLOCK), sl]
                    summed = summed + conv[at + taps - 1 - lag:at + taps - lag, sl] * jnp.where(
                        inside >= lag, far, 0.0
                    )
                sg = sigmoid(summed)
                active = summed * sg
                act_refs[d][lt, pl.ds(r0, BLOCK), :] = active
                if dsil_refs is not None:
                    dsil_refs[d][lt, pl.ds(r0, BLOCK), :] = sg + active * (1.0 - sg)

    over_rows(total, conv_rows)
    out = []
    for d in range(2):
        high, low = split(wide(act_refs[d]))
        sel = pack_ref[0:LANES, :]
        out.append(mm_nt(high, sel) + mm_nt(low, sel))
    return out


def own_front_kernel(dims, pack_ref, sigs_ref, pos_ref, rem_ref, act0_ref, act1_ref, dsil0_ref, dsil1_ref, part_ref,
                     ext_ref):
    parts = conv_silu(dims, 0, sigs_ref, pack_ref, pos_ref, rem_ref, (act0_ref, act1_ref), (dsil0_ref, dsil1_ref),
                      ext_ref)
    for d in range(2):
        part_ref[d] = parts[d]


def front_kernel(dims, *refs):
    n_ch, n_tok, rows, width, chans, inner, rank, states, taps = dims
    total = rows * n_ch
    nt = chans // LANES
    xd = rank + 2 * states
    packs = refs[:n_ch - 1]
    (sigs_ref, pos_ref, rem_ref, part_ref, stepw_hbm, sbias_hbm, picked_ref, stp0_ref, stp1_ref, sgm0_ref, sgm1_ref,
     ext_ref, stepw_pad_ref, pre_ref, act0_ref, act1_ref, stepw_ref, sbias_ref, sems) = refs[n_ch - 1:]
    stp_refs, sgm_refs = (stp0_ref, stp1_ref), (sgm0_ref, sgm1_ref)
    fetches = fetch_all((stepw_hbm, sbias_hbm), (stepw_ref, sbias_ref), sems)
    picked_ref[...] = part_ref[...]
    for k in range(1, n_ch):
        parts = conv_silu(dims, k, sigs_ref, packs[k - 1], pos_ref, rem_ref, (act0_ref, act1_ref), None, ext_ref)
        for d in range(2):
            picked_ref[d] += parts[d]
    for fetch in fetches:
        fetch.wait()
    stepw_pad_ref[...] = jnp.zeros_like(stepw_pad_ref)
    for d in range(2):
        base = d * xd
        stepw_pad_ref[d, base:base + rank, :] = stepw_ref[d]
        pre_ref[...] = mm3(mm, picked_ref[d], stepw_pad_ref[d]) + sbias_ref[d:d + 1, :]

        def step_rows(r0):
            for lt in range(nt):
                x = pre_ref[pl.ds(r0, BLOCK), tile(lt)]
                tail = jnp.exp(-jnp.abs(x))
                whole = 1.0 + tail
                inv = pltpu.reciprocal(whole, approx=True)
                inv = inv * (2.0 - whole * inv)
                small = tail * (1.0 - tail * (0.5 - tail * (1.0 / 3.0)))
                stp_refs[d][lt, pl.ds(r0, BLOCK), :] = jnp.maximum(x, 0.0) + jnp.where(
                    tail < 1e-3, small, jnp.log(whole)
                )
                sgm_refs[d][lt, pl.ds(r0, BLOCK), :] = jnp.where(x >= 0.0, inv, tail * inv)

        over_rows(total, step_rows)


def conv_rows_of(pack_ref, taps):
    return pack_ref[LANES:LANES + 16, :].astype(F32) + pack_ref[LANES + 16:LANES + 32, :].astype(F32)


def selectors(states):
    lanes = np.arange(states * LANES) >> 7
    column = np.arange(LANES)
    spread = ((column[:, None] % states) == lanes[None, :]) & (column[:, None] < 2 * states)
    gather = lanes[:, None] == column[None, :]
    return jnp.asarray(spread, LOW), jnp.asarray(gather, LOW)


def spread_maps(first, states, picked, lanes_ref, e_ref, dest):
    moved = pltpu.roll(picked, LANES - first, 1)
    high = moved.astype(LOW).astype(F32)
    low = pltpu.roll(moved - high, states, 1)
    spot = lax.broadcasted_iota(jnp.int32, moved.shape, 1)
    lanes_ref[...] = jnp.where(spot < states, high, jnp.where(spot < 2 * states, low, 0.0)).astype(LOW)

    dest[...] = mm(lanes_ref[...], e_ref[...])


def fill_rates(rate, nt, states, r2_ref):
    for lt in range(nt):
        for n in range(states):
            r2_ref[lt, n] = jnp.broadcast_to(rate[n:n + 1, tile(lt)] * LOG2E, (8, LANES))


def gate_kernel(dims, *refs):
    n_ch, n_tok, rows, width, chans, inner, rank, states, taps = dims
    total = rows * n_ch
    cots = refs[:n_ch]
    wout_ref, gate_ref, _, cotp_ref, gg_ref, gy_ref = refs[n_ch:]
    me = lax.axis_index("ch")
    for r0 in range(0, total, 256):
        cotp = 0.0
        for k in range(n_ch):
            moved = order_matrix(r0, 256, lax.rem(me + k, n_ch) * rows, rows, total)
            cotp = cotp + mm(moved, cots[k][...])
        cotp_ref[r0:r0 + 256, :] = cotp.astype(LOW)
    gg_ref[...] = mm_nt(cotp_ref[...], wout_ref[...]).astype(LOW)

    def gate_rows(r0):
        rr = pl.ds(r0, BLOCK)
        for lt in range(chans // LANES):
            gate = gate_ref[rr, tile(lt)].astype(F32)
            gy_ref[lt, rr, :] = gg_ref[rr, tile(lt)].astype(F32) * (gate * sigmoid(gate)) * 0.5

    over_rows(total, gate_rows)


def forward_kernel(dims, d, gy_ref, act_ref, stp_ref, picked_ref, dlog_ref, place_ref, e_ref, er_ref, *refs):
    n_ch, n_tok, rows, width, chans, inner, rank, states, taps = dims
    total = rows * n_ch
    length = total // 8
    nt = chans // LANES
    xd = rank + 2 * states
    first = d * xd + rank
    (y_ref, gains_ref, bb_ref, cb_ref, a_ref, h_ref, gmap_ref,
     r2_ref, lanes_ref, p_ref) = refs
    zero = jnp.zeros((8, LANES), F32)
    fill_rates(-jnp.exp(dlog_ref[d]), nt, states, r2_ref)
    spread_maps(first, states, picked_ref[d], lanes_ref, e_ref, bb_ref)
    spread_maps(first + states, states, picked_ref[d], lanes_ref, e_ref, cb_ref)
    p_ref[...] = jnp.zeros_like(p_ref)

    def along(j):
        return pl.multiple_of((length - 1 - j if d else j) * 8, 8)

    def scan_tile(lt, carry):
        def ends(j2, state):
            state, step_sum = list(state[:-1]), state[-1]
            at = [along(2 * j2 + jj) for jj in range(2)]
            sk, u = [], []
            for r0 in at:
                step = stp_ref[lt, pl.ds(r0, 8), :]
                sk.append(jnp.where(place_ref[pl.ds(r0, 8), :] == 0, HUGE_STEP, step))
                u.append(step * act_ref[lt, pl.ds(r0, 8), :])
            for n in range(states):
                for jj, r0 in enumerate(at):
                    a = jnp.exp2(sk[jj] * r2_ref[lt, n])
                    a_ref[lt, pl.ds(r0, 8), lane(n)] = a
                    state[n] = a * state[n] + u[jj] * bb_ref[pl.ds(r0, 8), lane(n)]
            return tuple(state) + (step_sum + (sk[0] + sk[1]),)

        out = over_pairs(length, ends, (zero,) * (states + 1))
        begin = []
        for n in range(states):
            whole_gain = jnp.exp2(out[-1] * r2_ref[lt, n])
            gains_ref[lt, n] = whole_gain
            begin.append(link_blocks(whole_gain, out[n], d == 0))

        def forward(j2, state):
            state = list(state)
            at = [along(2 * j2 + jj) for jj in range(2)]
            r16 = pl.multiple_of((length - 2 - 2 * j2 if d else 2 * j2) * 8, 16)
            u = [stp_ref[lt, pl.ds(r0, 8), :] * act_ref[lt, pl.ds(r0, 8), :] for r0 in at]
            gy = [gy_ref[lt, pl.ds(r0, 8), :] for r0 in at]
            sums = [[None, None], [None, None]]
            for n in range(states):
                prods = []
                for jj, r0 in enumerate(at):
                    h_ref[lt, pl.ds(r0, 8), lane(n)] = state[n]
                    state[n] = a_ref[lt, pl.ds(r0, 8), lane(n)] * state[n] + u[jj] * bb_ref[pl.ds(r0, 8), lane(n)]
                    term = state[n] * cb_ref[pl.ds(r0, 8), lane(n)]
                    sums[jj][n % 2] = term if sums[jj][n % 2] is None else sums[jj][n % 2] + term
                    prods.append(state[n] * gy[jj])
                p_ref[pl.ds(r16, 16), lane(n)] += jnp.concatenate(prods[::-1] if d else prods, axis=0).astype(LOW)
            for jj, r0 in enumerate(at):
                y_ref[lt, pl.ds(r0, 8), :] = sums[jj][0] + sums[jj][1]
            return tuple(state)

        over_pairs(length, forward, tuple(begin))
        return carry

    lax.fori_loop(0, nt, scan_tile, 0)
    gmap_ref[...] = pltpu.roll(mm(p_ref[...], er_ref[...]), first + states, 1)


def out_kernel(dims, y0_ref, y1_ref, act0_ref, act1_ref, skip_ref, gate_ref, gg_ref, normed_ref, cotp_ref, *refs):
    n_ch, n_tok, rows, width, chans, inner, rank, states, taps = dims
    total = rows * n_ch
    gated_ref, ggate_ref, own_ref, send_ref = refs

    def gate_back(r0):
        rr = pl.ds(r0, BLOCK)
        for lt in range(chans // LANES):
            sl = tile(lt)
            out = (
                y0_ref[lt, rr, :] + y1_ref[lt, rr, :]
                + skip_ref[0:1, sl] * act0_ref[lt, rr, :] + skip_ref[1:2, sl] * act1_ref[lt, rr, :]
            ) * 0.5
            gate = gate_ref[rr, sl].astype(F32)
            sg = sigmoid(gate)
            silu = gate * sg
            gated_ref[rr, sl] = (out * silu).astype(LOW)
            ggate_ref[rr, sl] = (gg_ref[rr, sl].astype(F32) * out * (sg + silu * (1.0 - sg))).astype(LOW)

    over_rows(total, gate_back)
    gated = gated_ref[...]
    gout = mm_tn(gated, cotp_ref[...])
    gin = mm_tn(normed_ref[...], ggate_ref[...])
    folded = [gout[:, i * chans:(i + 1) * chans] for i in range(width // chans)]
    pack(own_ref, send_ref, [folded, [gin]])


def block_kernel(dims, gated_ref, wout_ref, _, own_ref, *refs):
    n_ch, rows = dims[0], dims[2]
    part = mm(gated_ref[...], wout_ref[...])
    token_rows(lax.axis_index("ch"), part, n_ch, rows, rows * n_ch, own_ref, refs)


def token_rows(me, part, n_ch, rows, total, own_ref, other_refs):
    high, low = split(part)
    mine = take_tokens(me * rows, rows, total)
    own_ref[...] = mm(mine, high) + mm(mine, low)
    for k in range(1, n_ch):
        theirs = take_tokens(lax.rem(me + k, n_ch) * rows, rows, total)
        other_refs[k - 1][...] = mm(theirs, high).astype(LOW)


def my_place():
    tok = lax.axis_index("tok")
    return tok & 1, (tok >> 1) & 1


def pack(own_ref, send_ref, groups):
    core, near = my_place()
    runs = []
    at = 0
    for group in groups:
        total = sum(piece.shape[0] for piece in group)
        size = chunk_rows(PIECES, total)
        place = 0
        for piece in group:
            for i in range(0, piece.shape[0], 8):
                runs.append(divmod(place + i, size) + (at, piece[i:i + 8, :]))
            place += piece.shape[0]
        for i in range(place, size * PIECES, 8):
            runs.append(divmod(i, size) + (at, jnp.zeros((8, own_ref.shape[2]), F32)))
        at += size
    for side in range(2):
        @pl.when(core == side)
        def _():
            for p, r, base, rows in runs:
                slot = (p & 1) ^ near
                if p >> 1 == side:
                    own_ref[slot, base + r:base + r + 8, :] = rows
                else:
                    send_ref[slot, base + r:base + r + 8, :] = rows.astype(LOW)


def backward_kernel(dims, d, lt, n_wait, *refs):
    n_ch, n_tok, rows, width, chans, inner, rank, states, taps = dims
    total = rows * n_ch
    length = total // 8
    xd = rank + 2 * states
    base = d * xd
    first = base + rank
    sl = tile(lt)
    last_tile = lt == chans // LANES - 1
    refs = list(refs)

    def take(n):
        out = refs[:n]
        del refs[:n]
        return out

    (gy_ref, act_ref, stp_ref, sgm_ref, picked_ref, gains_ref, bb_ref, cb_ref, a_ref, h_ref, dlog_ref, skip_ref,
     stepw_ref, er_ref) = take(14)
    before = take(2)
    take(n_wait)
    gpick_ref, = take(1)
    if last_tile:
        low_ref, = take(1)
    else:
        q_ref, = take(1)
    gact_ref, gstepw_ref, gdlog_ref, misc_ref = take(4)
    if last_tile:
        q_ref, = take(1)
    r2_ref, gu_ref, gs_ref, gpre_ref, stepw_pad_ref = refs

    rate = -jnp.exp(dlog_ref[d, :, sl])
    for n in range(states):
        r2_ref[n] = jnp.broadcast_to(rate[n:n + 1] * LOG2E, (8, LANES))
    zero = jnp.zeros((8, LANES), F32)

    def against(j):
        return pl.multiple_of((j if d else length - 1 - j) * 8, 8)

    def ends_back(j2, state):
        state = list(state)
        at = [against(2 * j2 + jj) for jj in range(2)]
        gy = [gy_ref[lt, pl.ds(r0, 8), :] for r0 in at]
        for n in range(states):
            for jj, r0 in enumerate(at):
                state[n] = a_ref[lt, pl.ds(r0, 8), lane(n)] * (cb_ref[pl.ds(r0, 8), lane(n)] * gy[jj] + state[n])
        return tuple(state)

    back = over_pairs(length, ends_back, (zero,) * states)
    begin = [link_blocks(gains_ref[lt, n], back[n], d == 1) for n in range(states)]

    def backward(j2, state):
        grad, rate_sum = list(state[:states]), list(state[states:])
        at = [against(2 * j2 + jj) for jj in range(2)]
        r16 = pl.multiple_of((2 * j2 if d else length - 2 - 2 * j2) * 8, 16)
        gy = [gy_ref[lt, pl.ds(r0, 8), :] for r0 in at]
        step = [stp_ref[lt, pl.ds(r0, 8), :] for r0 in at]
        u = [step[jj] * act_ref[lt, pl.ds(r0, 8), :] for jj, r0 in enumerate(at)]
        gu = [[None, None], [None, None]]
        gs = [[None, None], [None, None]]
        for n in range(states):
            prods = []
            for jj, r0 in enumerate(at):
                g = cb_ref[pl.ds(r0, 8), lane(n)] * gy[jj] + grad[n]
                prods.append(g * u[jj])
                term = g * bb_ref[pl.ds(r0, 8), lane(n)]
                gu[jj][n % 2] = term if gu[jj][n % 2] is None else gu[jj][n % 2] + term
                grad[n] = a_ref[lt, pl.ds(r0, 8), lane(n)] * g
                q = grad[n] * h_ref[lt, pl.ds(r0, 8), lane(n)]
                rate_sum[n] = rate_sum[n] + q * step[jj]
                term = q * r2_ref[n]
                gs[jj][n % 2] = term if gs[jj][n % 2] is None else gs[jj][n % 2] + term
            value = jnp.concatenate(prods if d else prods[::-1], axis=0).astype(LOW)
            if lt:
                value = value + before[1][pl.ds(r16, 16), lane(n)]
            q_ref[pl.ds(r16, 16), lane(n)] = value
        for jj, r0 in enumerate(at):
            gu_ref[pl.ds(r0, 8), :] = gu[jj][0] + gu[jj][1]
            gs_ref[pl.ds(r0, 8), :] = gs[jj][0] + gs[jj][1]
        return tuple(grad) + tuple(rate_sum)

    last = over_pairs(length, backward, tuple(begin) + (zero,) * states)
    for n in range(states):
        gdlog_ref[n:n + 1, :] = jnp.sum(last[states + n], axis=0, keepdims=True) * rate[n:n + 1]
    misc_ref[...] = jnp.zeros_like(misc_ref)

    def post_rows(r0):
        rr = pl.ds(r0, BLOCK)
        active = act_ref[lt, rr, :]
        gu = gu_ref[rr, :]
        gy = gy_ref[lt, rr, :]
        gpre = (gs_ref[rr, :] * LN2 + gu * active) * sgm_ref[lt, rr, :]
        gpre_ref[rr, :] = gpre
        gact_ref[rr, :] = gu * stp_ref[lt, rr, :] + skip_ref[d:d + 1, sl] * gy
        misc_ref[0:1, :] += jnp.sum(gpre, axis=0, keepdims=True)
        misc_ref[1:2, :] += jnp.sum(gy * active, axis=0, keepdims=True)

    over_rows(total, post_rows)
    stepw_pad_ref[...] = jnp.zeros_like(stepw_pad_ref)
    stepw_pad_ref[base:base + rank, :] = stepw_ref[d, :, sl]
    gpre = gpre_ref[...]
    gpick = mm3(mm_nt, gpre, stepw_pad_ref[...]) + before[0][...]
    if last_tile:
        gpick = gpick + pltpu.roll(mm(q_ref[...], er_ref[...]), first, 1)
        low_ref[...] = gpick.astype(LOW)
    gpick_ref[...] = gpick
    gstepw_ref[...] = mm3(mm_tn, picked_ref[d], gpre)[base:base + rank, :]


def conv_back(dims, d, pos_ref, rem_ref, gpick_refs, gact_refs, act_ref, dsil_ref, sigs_ref, pack_ref, gsig_ref,
              gsel_ref, gconv_ref, gcp_ref, ext_ref, gcs_ref):
    n_ch, n_tok, rows, width, chans, inner, rank, states, taps = dims
    total = rows * n_ch
    nt = chans // LANES
    halo = 8 * (taps - 1)
    xd = rank + 2 * states
    gpick = gpick_refs[0][...]
    for k in range(1, n_ch):
        gpick = gpick + gpick_refs[k][...].astype(F32)
    spot = lax.broadcasted_iota(jnp.int32, (total, LANES), 1)
    gpick = jnp.where((spot >= d * xd) & (spot < (d + 1) * xd), gpick, 0.0)
    high, low = split(gpick)
    sel = pack_ref[0:LANES, :]
    gcp_ref[pl.ds(halo, total), :] = mm(high, sel) + mm(low, sel)
    gsel_ref[...] = mm3(mm_tn, gpick, wide(act_ref))[d * xd:(d + 1) * xd, :]
    ext_ref[pl.ds(halo, total), :] = sigs_ref[0].astype(F32)
    halo_fill(ext_ref, total, halo, slice(None))
    gcs_ref[...] = jnp.zeros_like(gcs_ref)
    conv = conv_rows_of(pack_ref, taps)

    def fold8(x):
        out = x[0:8]
        for i in range(8, BLOCK, 8):
            out = out + x[i:i + 8]
        return out

    def conv_rows(r0):
        rr = pl.ds(r0, BLOCK)
        inside = rem_ref[rr, :] if d else pos_ref[rr, :]
        for lt in range(nt):
            sl = tile(lt)
            gc = (gcp_ref[pl.ds(r0 + halo, BLOCK), sl] + gact_refs[lt][rr, :]) * dsil_ref[lt, rr, :]
            gcp_ref[pl.ds(r0 + halo, BLOCK), sl] = gc
            gcs_ref[taps, :, sl] += fold8(gc)
            gcs_ref[taps - 1, :, sl] += fold8(gc * ext_ref[pl.ds(r0 + halo, BLOCK), sl])
            for lag in range(1, taps):
                far = ext_ref[pl.ds(r0 + (halo + 8 * lag if d else halo - 8 * lag), BLOCK), sl]
                gcs_ref[taps - 1 - lag, :, sl] += fold8(jnp.where(inside >= lag, gc * far, 0.0))

    over_rows(total, conv_rows)
    halo_fill(gcp_ref, total, halo, slice(None))

    def signal_rows(r0):
        rr = pl.ds(r0, BLOCK)
        inside = pos_ref[rr, :] if d else rem_ref[rr, :]
        for lt in range(nt):
            sl = tile(lt)
            at = d * (taps + 1)
            summed = conv[at + taps - 1:at + taps, sl] * gcp_ref[pl.ds(r0 + halo, BLOCK), sl]
            for lag in range(1, taps):
                far = gcp_ref[pl.ds(r0 + (halo - 8 * lag if d else halo + 8 * lag), BLOCK), sl]
                summed = summed + conv[at + taps - 1 - lag:at + taps - lag, sl] * jnp.where(inside >= lag, far, 0.0)
            gsig_ref[rr, sl] = summed

    over_rows(total, signal_rows)
    gconv_ref[...] = jnp.zeros_like(gconv_ref)
    for k in range(taps + 1):
        gconv_ref[k:k + 1, :] = jnp.sum(gcs_ref[k], axis=0, keepdims=True)


def first_conv_kernel(dims, n_wait, pos_ref, rem_ref, *refs):
    n_ch, nt = dims[0], dims[4] // LANES
    gpicks, gacts, refs = refs[:n_ch], refs[n_ch:n_ch + nt], refs[n_ch + nt:]
    conv_back(dims, 0, pos_ref, rem_ref, gpicks, gacts, *refs[:4], *refs[4 + n_wait:])


def second_conv_kernel(dims, pos_ref, rem_ref, *refs):
    n_ch, n_tok, rows, width, chans, inner, rank, states, taps = dims
    nt = chans // LANES
    refs = list(refs)

    def take(n):
        out = refs[:n]
        del refs[:n]
        return out

    gpicks, gacts, rest, _ = take(n_ch), take(nt), take(4), take(2)
    gsig0_ref, gsel0_ref, gconv0_ref, normed_ref, ggate_ref, xp_ref, win_ref = take(7)
    tiles = [[take(3) for _ in range(nt)] for _ in range(2)]
    (gsig_ref, own_ref, send_ref, gcp_ref, ext_ref, gcs_ref, gsum_ref, gsel_ref, gconv_ref, small_ref, gain_ref) = refs
    conv_back(dims, 1, pos_ref, rem_ref, gpicks, gacts, *rest, gsum_ref, gsel_ref, gconv_ref, gcp_ref, ext_ref,
              gcs_ref)
    me = lax.axis_index("ch")
    gsig = (gsum_ref[...] + gsig0_ref[...]).astype(LOW)
    gsig_ref[...] = gsig
    gn = grad_normed(dims, me, gsig, ggate_ref, win_ref)
    xp = xp_ref[...].astype(F32)
    scale = lax.rsqrt(jnp.mean(xp * xp, axis=1, keepdims=True) + norm_eps)
    ggain = jnp.sum(gn * xp * scale, axis=0, keepdims=True)
    gin = mm_tn(normed_ref[...], gsig)
    places = small_places(dims)
    small_ref[...] = jnp.zeros_like(small_ref)
    xd = rank + 2 * states
    for d in range(2):
        at = places["select"] + d * xd
        small_ref[at:at + xd, :] = (gsel0_ref, gsel_ref)[d][...]
        conv_ref = (gconv0_ref, gconv_ref)[d]
        at = places["taps"] + d * taps
        small_ref[at:at + taps, :] = conv_ref[0:taps, :]
        small_ref[places["bias"] + d:places["bias"] + d + 1, :] = conv_ref[taps:taps + 1, :]
        for lt in range(nt):
            gstepw_ref, gdlog_ref, misc_ref = tiles[d][lt]
            sl = tile(lt)
            at = places["step"] + d * rank
            small_ref[at:at + rank, sl] = gstepw_ref[...]
            at = places["decay"] + d * states
            small_ref[at:at + states, sl] = gdlog_ref[...]
            small_ref[places["sbias"] + d:places["sbias"] + d + 1, sl] = misc_ref[0:1, :]
            small_ref[places["skip"] + d:places["skip"] + d + 1, sl] = misc_ref[1:2, :]
    gain_ref[...] = jnp.zeros_like(gain_ref)
    for i in range(width // chans):
        gain_ref[i:i + 1, :] = ggain[:, i * chans:(i + 1) * chans]
    pack(own_ref, send_ref, [[gin], [gain_ref[...]], [small_ref[...]]])


def grad_normed(dims, me, gsig, ggate_ref, win_ref):
    n_ch, n_tok, rows, width, chans, inner, rank, states, taps = dims
    return mm_nt(gsig, win_ref[:, pl.ds(pl.multiple_of(me * chans, LANES), chans)]) + mm_nt(
        ggate_ref[...], win_ref[:, pl.ds(pl.multiple_of(inner + me * chans, LANES), chans)]
    )


def normed_kernel(dims, gsig_ref, ggate_ref, win_ref, *refs):
    n_ch, n_tok, rows, width, chans, inner, rank, states, taps = dims
    blk_refs, gn_own_ref, part_refs = refs[:n_ch - 1], refs[n_ch - 1], refs[n_ch:]
    me = lax.axis_index("ch")
    gn = grad_normed(dims, me, gsig_ref[...], ggate_ref, win_ref)
    token_rows(me, gn, n_ch, rows, rows * n_ch, gn_own_ref, [ref.at[rows:2 * rows] for ref in part_refs])
    for blk_ref, part_ref in zip(blk_refs, part_refs):
        part_ref[0:rows, :] = blk_ref[...]


def small_places(dims):
    n_ch, n_tok, rows, width, chans, inner, rank, states, taps = dims
    places, at = {}, 0
    for name, size in (
        ("select", 2 * (rank + 2 * states)), ("step", 2 * rank), ("decay", 2 * states), ("taps", 2 * taps),
        ("bias", 2), ("sbias", 2), ("skip", 2),
    ):
        places[name] = at
        at += size
    places["end"] = round_up(at, 8)
    return places


def token_kernel(n_ch, at, tok_ref, cot_ref, gain_ref, blk_ref, gn_ref, *refs):
    parts = refs[:n_ch - 1]
    out_ref, gtok_ref, mark_ref = refs[n_ch - 1:]
    mark_ref[...] = jnp.zeros_like(mark_ref)
    tokens = tok_ref[...].astype(F32)
    out = tokens + blk_ref[...]
    gn = gn_ref[...]
    rows = tok_ref.shape[0]
    for part in parts:
        out = out + part[at:at + rows, :].astype(F32)
        gn = gn + part[at + rows:at + 2 * rows, :].astype(F32)
    out_ref[...] = out.astype(LOW)
    scale = lax.rsqrt(jnp.mean(tokens * tokens, axis=1, keepdims=True) + norm_eps)
    unit = tokens * scale
    scaled = gn * gain_ref[...][None, :]
    gtok_ref[...] = cot_ref[...].astype(F32) + scale * (
        scaled - unit * jnp.mean(scaled * unit, axis=1, keepdims=True)
    )


def join_kernel(n_ch, rb, base_ref, *refs):
    others, out_ref = refs[:n_ch - 1], refs[-1]
    out_ref[0:rb, :] = base_ref[0:rb, :]
    mixed = base_ref[rb:rb + 16, :].astype(F32)
    gain = mixed[0:8]
    for c, other in enumerate(others):
        out_ref[(c + 1) * rb:(c + 2) * rb, :] = other[0:rb, :]
        gain = gain + other[rb:rb + 16, :].astype(F32)[0:8]
    at = n_ch * rb
    out_ref[at:at + 16, :] = jnp.concatenate([gain, mixed[8:16]], axis=0).astype(LOW)
    out_ref[at + 16:, :] = base_ref[rb + 16:, :]


def my_pieces():
    core, near = my_place()
    return [(core ^ (k >> 1)) * 2 + (near ^ (k & 1)) for k in range(PIECES)]


def place_columns(dims, every, at, block_ref, gin_hbm, first, sems):
    n_ch, n_tok, rows, width, chans, inner, rank, states, taps = dims
    rb = chunk_rows(PIECES, width)
    me = lax.axis_index("ch")
    copies = []
    for k, piece in enumerate(my_pieces()):
        rr = pl.ds(pl.multiple_of(piece * rb, 8), rb)
        for c in range(n_ch):
            j = lax.rem(me + c, n_ch) * chans
            block_ref[k, :, pl.ds(pl.multiple_of(j, LANES), chans)] = every[k][
                at + c * rb:at + (c + 1) * rb, :
            ].astype(F32)
        copies.append(pltpu.make_async_copy(block_ref.at[k], gin_hbm.at[rr, first:first + inner], sems.at[k]))
        copies[-1].start()
    return copies


def early_result_kernel(dims, every_ref, gin_hbm, gout_hbm, mark_ref, block_ref, gout_ref, sems):
    n_ch, n_tok, rows, width, chans, inner, rank, states, taps = dims
    ra = chunk_rows(PIECES, chans)
    copies = place_columns(dims, [every_ref.at[k] for k in range(PIECES)], ra, block_ref, gin_hbm, inner, sems)
    for k, piece in enumerate(my_pieces()):
        gout_ref[pl.ds(pl.multiple_of(piece * ra, 8), ra), :] = every_ref[k, 0:ra, :].astype(F32)
    mark_ref[...] = jnp.zeros_like(mark_ref)
    copies.append(pltpu.make_async_copy(gout_ref, gout_hbm, sems.at[PIECES]))
    copies[-1].start()
    for copy in copies:
        copy.wait()


def late_result_kernel(dims, *refs):
    every, gin_hbm, refs = refs[:PIECES], refs[PIECES + 1], refs[PIECES + 2:]
    n_ch, n_tok, rows, width, chans, inner, rank, states, taps = dims
    outs, stages, (small_ref, block_ref, sems) = refs[:8], refs[8:16], refs[16:]
    ggain_ref, gtaps_ref, gbias_ref, gsel_ref, gstep_ref, gsbias_ref, gdecay_ref, gskip_ref = stages
    places = small_places(dims)
    rb, rs = chunk_rows(PIECES, width), chunk_rows(PIECES, places["end"])
    at = n_ch * rb
    gain = 0.0
    for k, piece in enumerate(my_pieces()):
        mixed = every[k][at:at + 8 + rs, :].astype(F32)
        small_ref[pl.ds(pl.multiple_of(piece * rs, 8), rs), :] = mixed[8:]
        gain = gain + mixed[0:8]
    ggain_ref[...] = gain[0]
    xd = rank + 2 * states
    for d in range(2):
        for ref, name, size in ((gsel_ref, "select", xd), (gstep_ref, "step", rank), (gdecay_ref, "decay", states),
                                (gtaps_ref, "taps", taps)):
            first = places[name] + d * size
            ref[d] = small_ref[first:first + size, :]
    for ref, name in ((gbias_ref, "bias"), (gsbias_ref, "sbias"), (gskip_ref, "skip")):
        ref[...] = small_ref[places[name]:places[name] + 2, :]
    copies = [pltpu.make_async_copy(a, b, sems.at[PIECES + i]) for i, (a, b) in enumerate(zip(stages, outs))]
    for copy in copies:
        copy.start()
    copies += place_columns(dims, every, 0, block_ref, gin_hbm, 0, sems)
    for copy in copies:
        copy.wait()


def chunk_rows(n_tok, total):
    return round_up(-(-total // n_tok), 8)


def vmem_specs(n):
    return [pl.BlockSpec(memory_space=pltpu.VMEM)] * n


def kernel_call(kernel, name, operands, outs, scratch, limit, us, places=(), hbm_outs=(), aliases=()):
    specs = vmem_specs(len(operands))
    for i, space in places:
        specs[i] = pl.BlockSpec(memory_space=space)
    return pl.pallas_call(
        kernel,
        name=name,
        out_shape=outs,
        in_specs=specs,
        out_specs=[pl.BlockSpec(memory_space=pl.ANY if i in hbm_outs else pltpu.VMEM) for i in range(len(outs))],
        scratch_shapes=scratch,
        input_output_aliases=dict(aliases),
        compiler_params=pltpu.CompilerParams(vmem_limit_bytes=limit * 1024 * 1024),
        cost_estimate=pl.CostEstimate(flops=int(us * 1e7), bytes_accessed=int(us * 3e4), transcendentals=0),
    )(*operands)


def rotated(x, n_ch):
    return [x] + [
        lax.ppermute(x, "ch", [((i + k) % n_ch, i) for i in range(n_ch)]) for k in range(1, n_ch)
    ]


def sent(parts, n_ch):
    return [
        lax.ppermute(parts[k - 1], "ch", [(i, (i + k) % n_ch) for i in range(n_ch)]) for k in range(1, n_ch)
    ]


def partner_pairs(n_tok, stride):
    return [(i, i ^ stride) for i in range(n_tok)]


def swap(x, n_tok, stride):
    return lax.ppermute(x, "tok", partner_pairs(n_tok, stride))


def near_strides():
    return [1, 2]


def far_strides(n_tok):
    strides, s = [], 4
    while s < n_tok:
        strides.append(s)
        s *= 2
    return strides


def add_kernel(halving, last, own_ref, got_ref, *refs):
    send_ref = refs[-1]
    if halving:
        refs[-2][...] = own_ref[0] + got_ref[0].astype(F32)
        send_ref[...] = (own_ref[1] + got_ref[1].astype(F32)).astype(LOW)
    else:
        both = own_ref[...] + got_ref[...].astype(F32)
        send_ref[...] = both.astype(LOW)
        if not last:
            refs[-2][...] = both


class Reduction:
    def __init__(self, own, send, n_tok, limit):
        self.own, self.n_tok, self.limit = own, n_tok, limit
        self.strides = [2] + far_strides(n_tok)
        self.got = swap(send, n_tok, 1)

    def done(self):
        return self.own.dtype == LOW

    def add(self, *wait):
        halving, last = self.own.ndim == 3, not self.strides
        shape = self.own.shape[-2:]
        outs = kernel_call(
            functools.partial(add_kernel, halving, last), "add_kernel", (self.own, self.got, *wait),
            ([] if last else [jax.ShapeDtypeStruct(shape, F32)]) + [jax.ShapeDtypeStruct(shape, LOW)], [], self.limit,
            0.1, [(i, pl.ANY) for i in range(2, 2 + len(wait))],
        )
        self.own = outs[0]
        if not last:
            self.got = swap(outs[1], self.n_tok, self.strides.pop(0))


def stack_kernel(spans, *refs):
    at = 0
    for (first, rows), ref in zip(spans, refs):
        refs[-1][at:at + rows, :] = ref[first:first + rows, :]
        at += rows


def stack(parts, wait, limit):
    parts = [part if isinstance(part, tuple) else (part, 0, part.shape[0]) for part in parts]
    arrays, spans = [part[0] for part in parts], [part[1:] for part in parts]
    shape = (sum(rows for _, rows in spans), arrays[0].shape[1])
    return kernel_call(
        functools.partial(stack_kernel, spans), "stack_kernel", (*arrays, wait), [jax.ShapeDtypeStruct(shape, LOW)], [],
        limit, 0.1, [(len(parts), pl.ANY)],
    )[0]


def local(
    tokens,
    cotangent,
    norm_gain,
    in_proj,
    conv_weight,
    conv_bias,
    select_proj,
    step_proj,
    step_bias,
    decay_log,
    skip_gain,
    out_proj,
    clip_lengths,
):
    n_ch, n_tok = lax.axis_size("ch"), lax.axis_size("tok")
    rows, width = tokens.shape
    real = conv_bias.shape[1]
    taps, rank, states = conv_weight.shape[1], step_proj.shape[1], decay_log.shape[1]
    chans = round_up(real, LANES)
    extra = chans - real
    xd = rank + 2 * states

    def pad_last(x):
        return jnp.pad(x, [(0, 0)] * (x.ndim - 1) + [(0, extra)]) if extra else x

    if extra:
        in_proj = pad_last(in_proj.reshape(width, 2 * n_ch, real)).reshape(width, 2 * n_ch * chans)
        step_proj, step_bias, decay_log, skip_gain = map(pad_last, (step_proj, step_bias, decay_log, skip_gain))
        out_proj = jnp.pad(out_proj, ((0, extra), (0, 0)))
    inner = n_ch * chans
    total = rows * n_ch
    nt = chans // LANES
    span = states * LANES
    halo = 8 * (taps - 1)
    fold = width // chans
    dims = (n_ch, n_tok, rows, width, chans, inner, rank, states, taps)
    limit = 16 if total <= 256 else 60
    shape = jax.ShapeDtypeStruct
    vm = pltpu.VMEM
    one = (nt, total, LANES)
    dma = pltpu.SemaphoreType.DMA
    spot = shape((total, LANES), jnp.int32)

    def far(*arrays):
        return [pltpu.with_memory_space_constraint(x, pltpu.HBM) for x in arrays]

    tok_parts = rotated(tokens, n_ch)
    (packed,) = kernel_call(
        functools.partial(weight_kernel, dims), "weight_kernel",
        far(select_proj.transpose(0, 2, 1), conv_weight, conv_bias), [shape((LANES + 32, chans), LOW)],
        [vm((2, xd, real), F32), vm((2, taps, real), F32), vm((2, real), F32), dma((3,))], limit, 20,
        [(i, pltpu.HBM) for i in range(3)],
    )
    pack_parts = rotated(packed, n_ch)
    fetched = (in_proj, tokens, norm_gain, cotangent)
    win, own, gain, cot_own = kernel_call(
        functools.partial(fetch_kernel, len(fetched)), "fetch_kernel", (*far(*fetched), packed),
        [shape(x.shape, x.dtype) for x in fetched], [dma((FETCHES + len(fetched) - 1,))], limit, 20,
        [(i, pltpu.HBM) for i in range(len(fetched))] + [(len(fetched), pl.ANY)],
    )
    normed, xp, sigs, gate, pos, rem = kernel_call(
        functools.partial(norm_kernel, dims), "norm_kernel",
        (*far(clip_lengths), own, gain, win, *tok_parts[1:]),
        [shape((total, width), LOW), shape((total, width), LOW), shape((n_ch, total, chans), LOW),
         shape((total, chans), LOW), spot, spot],
        [pltpu.SMEM(clip_lengths.shape, jnp.int32), dma], limit, 50, [(0, pltpu.HBM)],
    )
    cot_parts = rotated(cot_own, n_ch)
    ext = vm((total + 2 * halo, chans), F32)
    act0, act1, dsil0, dsil1, part = kernel_call(
        functools.partial(own_front_kernel, dims), "own_front_kernel", (packed, sigs, pos, rem),
        [shape(one, F32)] * 4 + [shape((2, total, LANES), F32)], [ext], limit, 1,
    )
    picked, stp0, stp1, sgm0, sgm1 = kernel_call(
        functools.partial(front_kernel, dims), "front_kernel",
        (*pack_parts[1:], sigs, pos, rem, part, *far(step_proj, step_bias)),
        [shape((2, total, LANES), F32)] + [shape(one, F32)] * 4,
        [ext, vm((2, LANES, chans), F32), vm((total, chans), F32), vm(one, F32), vm(one, F32),
         vm((2, rank, chans), F32), vm((2, chans), F32), dma((2,))],
        limit, 1, ((n_ch + 3, pltpu.HBM), (n_ch + 4, pltpu.HBM)),
    )

    ra, rb = chunk_rows(PIECES, chans * fold), chunk_rows(PIECES, width)
    r1 = ra + rb
    cotp, gg, gy = kernel_call(
        functools.partial(gate_kernel, dims), "gate_kernel", (*cot_parts, out_proj, gate, picked),
        [shape((total, width), LOW), shape((total, chans), LOW), shape(one, F32)], [], limit, 1,
        [(n_ch + 2, pl.ANY)],
    )
    spread, gather = selectors(states)
    scans = []
    for d, (act, stp) in enumerate(((act0, stp0), (act1, stp1))):
        scans.append(kernel_call(
            functools.partial(forward_kernel, dims, d), "forward_kernel_%d" % d,
            (gy, act, stp, picked, decay_log, rem if d else pos, spread, gather),
            [shape(one, F32), shape((nt, states, 8, LANES), F32)] + [shape((total, span), F32)] * 2
            + [shape((nt, total, span), F32)] * 2 + [shape((total, LANES), F32)],
            [vm((nt, states, 8, LANES), F32), vm((total, LANES), LOW), vm((total, span), LOW)],
            limit, 1,
        ))
    outs = kernel_call(
        functools.partial(out_kernel, dims), "out_kernel",
        (scans[0][0], scans[1][0], act0, act1, skip_gain, gate, gg, normed, cotp),
        [shape((total, chans), LOW), shape((total, chans), LOW), shape((2, r1, chans), F32),
         shape((2, r1, chans), LOW)],
        [], limit, 1,
    )
    gated, ggate, own1, send1 = outs

    early = Reduction(own1, send1, n_tok, limit)
    gpick_parts, gacts, tile_outs = [], [], [[], []]
    for d, (act, stp, sgm) in enumerate(((act0, stp0, sgm0), (act1, stp1, sgm1))):
        gains, bb, cb, decays, before_states, gmap = scans[d][1:]
        before = (gmap, gmap)
        gacts.append([])
        for lt in range(nt):
            final = lt == nt - 1
            operands = (gy, act, stp, sgm, picked, gains, bb, cb, decays, before_states, decay_log, skip_gain,
                        step_proj, gather, *before)
            wait = [early.own] if (d, lt) in ((1, 0), (1, nt - 1)) else []
            outs = kernel_call(
                functools.partial(backward_kernel, dims, d, lt, len(wait)), "backward_kernel_%d%d" % (d, lt),
                (*operands, *wait),
                [shape((total, LANES), F32)]
                + ([shape((total, LANES), LOW)] if final else [shape((total, span), LOW)])
                + [shape((total, LANES), F32), shape((rank, LANES), F32), shape((states, LANES), F32),
                   shape((8, LANES), F32)],
                ([vm((total, span), LOW)] if final else [])
                + [vm((states, 8, LANES), F32), vm((total, LANES), F32), vm((total, LANES), F32),
                   vm((total, LANES), F32), vm((LANES, LANES), F32)],
                limit, 0.5, [(len(operands) + i, pl.ANY) for i in range(len(wait))],
            )
            before = tuple(outs[:2])
            gacts[d].append(outs[2])
            tile_outs[d].extend(outs[-3:])
            if early.strides and (d, lt) in ((0, 0), (0, nt - 1), (1, nt - 2)):
                early.add(outs[-1])
        gpick_parts.append([outs[0]] + rotated(outs[1], n_ch)[1:])

    wait = [tile_outs[1][-1]]
    conv_scratch = [vm((total + 2 * halo, chans), F32), vm((total + 2 * halo, chans), F32),
                    vm((taps + 1, 8, chans), F32)]
    operands = (pos, rem, *gpick_parts[0], *gacts[0], act0, dsil0, sigs, packed, *wait)
    gsig0, gsel0, gconv0 = kernel_call(
        functools.partial(first_conv_kernel, dims, len(wait)), "first_conv_kernel", operands,
        [shape((total, chans), F32), shape((xd, chans), F32), shape((8, chans), F32)],
        conv_scratch, limit, 0.5, [(i, pl.ANY) for i in range(len(operands) - len(wait), len(operands))],
    )
    outs = kernel_call(
        functools.partial(block_kernel, dims), "block_kernel", (gated, out_proj, gconv0),
        [shape((rows, width), F32)] + [shape((rows, width), LOW)] * (n_ch - 1), [], limit, 0.5, [(2, pl.ANY)],
    )
    blk_own, blk_parts = outs[0], outs[1:]
    places = small_places(dims)
    rs = chunk_rows(PIECES, places["end"])
    r2 = rs + rb + 8
    gsig, own2, send2 = kernel_call(
        functools.partial(second_conv_kernel, dims), "second_conv_kernel",
        (pos, rem, *gpick_parts[1], *gacts[1], act1, dsil1, sigs, packed, blk_own, early.got, gsig0, gsel0, gconv0, normed, ggate, xp,
         win, *tile_outs[0], *tile_outs[1]),
        [shape((total, chans), LOW), shape((2, r2, chans), F32), shape((2, r2, chans), LOW)],
        conv_scratch + [vm((total, chans), F32), vm((xd, chans), F32), vm((8, chans), F32),
                        vm((places["end"], chans), F32), vm((8, chans), F32)],
        limit, 0.5, [(6 + n_ch + nt, pl.ANY), (7 + n_ch + nt, pl.ANY)],
    )
    outs = kernel_call(
        functools.partial(normed_kernel, dims), "normed_kernel", (gsig, ggate, win, *blk_parts),
        [shape((rows, width), F32)] + [shape((2 * rows, width), LOW)] * (n_ch - 1), [], limit, 0.5,
    )
    gn_own, token_parts = outs[0], outs[1:n_ch]

    late = Reduction(own2, send2, n_tok, limit)
    early.add(gn_own)
    while not early.done():
        early.add()
    gate = (early.own, ra, rb)
    if n_ch == 2 and width == chans:
        token_got = gates = sent([stack([gate, token_parts[0]], gn_own, limit)], n_ch)
    else:
        token_got, gates = sent(token_parts, n_ch), rotated(early.own[ra:], n_ch)[1:]
    late.add(gn_own)
    late.add()
    block_out, grad_tokens, mark = kernel_call(
        functools.partial(token_kernel, n_ch, token_got[0].shape[0] - 2 * rows), "token_kernel",
        (own, cot_own, gain, blk_own, gn_own, *token_got),
        [shape((rows, width), LOW), shape((rows, width), F32), shape((8, LANES), F32)], [], limit, 0.5,
    )
    early_piece = stack([early.own, *((got, 0, rb) for got in gates)], mark, limit)
    first_got = swap(early_piece, n_tok, 2)
    late.add(mark)
    while not late.done():
        late.add()
    early_pair = stack([early_piece, first_got], late.own, limit).reshape(2, ra + n_ch * rb, chans)
    every1 = jnp.concatenate([early_pair, swap(early_pair, n_tok, 1)], axis=0)
    assert rb % 16 == 0 and (rs + 8) % 16 == 0
    shared = late.own[:rb + 16]
    sides = [[], []]
    for side in range(2):
        for c in range(n_ch):
            if (side, c) == (0, 0):
                sides[0].append(late.own)
                continue
            pairs = [
                ((i ^ (2 * side)) * n_ch + (j + c) % n_ch, i * n_ch + j) for i in range(n_tok) for j in range(n_ch)
            ]
            sides[side].append(lax.ppermute(shared if c else late.own, ("tok", "ch"), pairs))

    def join(wait):
        mine = [
            kernel_call(
                functools.partial(join_kernel, n_ch, rb), "join_kernel", (*parts, wait),
                [shape((n_ch * rb + 8 + rs, chans), LOW)], [], limit, 0.5, [(n_ch, pl.ANY)],
            )[0] for parts in sides
        ]
        return mine + [swap(piece, n_tok, 1) for piece in mine]

    if not extra and fold == 1 and ra * PIECES == chans and rb * PIECES == width:
        block = vm((PIECES, rb, inner), F32)
        gin, gout, mark = kernel_call(
            functools.partial(early_result_kernel, dims), "early_result_kernel", (every1,),
            [shape((width, 2 * inner), F32), shape((chans, width), F32), shape((8, LANES), F32)],
            [block, vm((chans, width), F32), dma((PIECES + 1,))], limit, 2, hbm_outs=(0, 1),
        )
        every2 = join(mark)
        small_shapes = [(width,), (2, taps, chans), (2, chans), (2, xd, chans), (2, rank, chans), (2, chans),
                        (2, states, chans), (2, chans)]
        gin, ggain, gtaps, gbias, gsel, gstep, gsbias, gdecay, gskip = kernel_call(
            functools.partial(late_result_kernel, dims), "late_result_kernel",
            (*every2, gin),
            [shape((width, 2 * inner), F32)] + [shape(x, F32) for x in small_shapes],
            [vm(x, F32) for x in small_shapes] + [vm((rs * PIECES, chans), F32), block, dma((PIECES + 8,))], limit, 2,
            [(PIECES, pl.ANY)], hbm_outs=range(9), aliases={PIECES: 0},
        )
    else:
        every2 = jnp.stack(join(late.own))
        me, tok = lax.axis_index("ch"), lax.axis_index("tok")
        mine = (tok & 1) * 2 + ((tok >> 1) & 1)
        at = jnp.arange(PIECES) ^ mine
        every1, every2 = every1[at], every2[at]
        turn = (jnp.arange(n_ch) - me) % n_ch
        gate = every1[:, ra:].reshape(PIECES, n_ch, rb, chans)
        signal = every2[:, :n_ch * rb].reshape(PIECES, n_ch, rb, chans)
        gin = jnp.concatenate([signal[:, turn], gate[:, turn]], axis=1).transpose(0, 2, 1, 3)[..., :real]
        gin = gin.reshape(PIECES * rb, 2 * n_ch * real)[:width].astype(F32)
        gout = every1[:, :ra].reshape(PIECES * ra, chans)[:chans * fold]
        gout = jnp.concatenate([gout[i * chans:(i + 1) * chans] for i in range(fold)], axis=1)[:real].astype(F32)
        small = every2[:, n_ch * rb + 8:].reshape(PIECES * rs, chans).astype(F32)
        ggain = jnp.sum(every2[:, n_ch * rb:n_ch * rb + 8].astype(F32), axis=0)[:fold].reshape(width)

        def rows_of(name, size):
            return small[places[name]:places[name] + size]

        gsel, gstep, gdecay, gtaps = (
            rows_of(name, 2 * size).reshape(2, size, chans)[..., :real]
            for name, size in (("select", xd), ("step", rank), ("decay", states), ("taps", taps))
        )
        gbias, gsbias, gskip = (rows_of(name, 2)[:, :real] for name in ("bias", "sbias", "skip"))
    return (
        block_out,
        grad_tokens,
        ggain,
        gin,
        gtaps,
        gbias,
        gsel.transpose(0, 2, 1),
        gstep,
        gsbias,
        gdecay,
        gskip,
        gout,
    )


def solution(mesh):
    return jax.shard_map(
        local,
        mesh=mesh,
        in_specs=(
            P(("tok", "ch"), None),
            P(("tok", "ch"), None),
            P(),
            P(),
            P(None, None, "ch"),
            P(None, "ch"),
            P(None, "ch", None),
            P(None, None, "ch"),
            P(None, "ch"),
            P(None, None, "ch"),
            P(None, "ch"),
            P("ch", None),
            P("tok", None),
        ),
        out_specs=(
            P(("tok", "ch"), None),
            P(("tok", "ch"), None),
            P(),
            P(),
            P(None, None, "ch"),
            P(None, "ch"),
            P(None, "ch", None),
            P(None, None, "ch"),
            P(None, "ch"),
            P(None, None, "ch"),
            P(None, "ch"),
            P("ch", None),
        ),
        check_vma=False,
    )
```

time: 2870 us -> 84 us (0.03); the launches traced: 2830 us -> 83.9 us
  other arithmetic: 2050 us -> 0.1 us
  waiting for transfers between devices: 343 us -> 19.3 us
  local copies, waits for them, and re-layouts: 316 us -> 0.05 us
  blocking collectives: 50.4 us -> 0 us
  Pallas kernels: 0 us -> 39.8 us
    reduce_sum x420 -> x0, other arithmetic: 1620 us -> none  [the longest x400 1600 us: run_block(): results[row] = jnp.sum(carry * output_rows[row][:, None], axis=0)]
    add_any x18 -> x0, other arithmetic: 335 us -> none  [the longest x16 332 us: blocked_states(): lax.scan(jax.checkpoint(run_block), start, items, reverse=reverse)]
    psum x5 -> x0, waiting for transfers between devices: 324 us -> none  [the longest x2 144 us: local(): lax.psum((stack_pair(front_grads_ahead, front_grads_behind, 1), stack_pai...]
    slice x156 -> x1, local copies, waits for them, and re-layouts: 95.7 us -> 0.01 us  [local(): shared = late.own[:rb + 16]]
    squeeze x80 -> x0, local copies, waits for them, and re-layouts: 60.4 us -> none  [blocked_states(): lax.scan(jax.checkpoint(run_block), start, items, reverse=reverse)]
    another operation x573 -> x0, local copies, waits for them, and re-layouts: 58.6 us -> none  [the longest x560 48.7 us: run_block(): return (carry, jnp.stack(results))]
    dynamic_update_slice x80 -> x0, other arithmetic: 56.9 us -> none  [blocked_states(): lax.scan(jax.checkpoint(run_block), start, items, reverse=reverse)]
    mul x120 -> x0, local copies, waits for them, and re-layouts: 47.4 us -> none  [the longest x64 28.8 us: run_block(): (step_rows[row] * active_rows[row])[None, :] * input_rows[row][:, None]]
  transfers between devices with their start and end apart: 10 -> 21, of which waited for: 8 -> 10; matrix products, arithmetic and copies ran while one was open for 1% -> 0% of each run, Pallas kernels for 0% -> 29%
where the time goes in v1:
time: 84 us; the launch traced here: 83.9 us
  Pallas kernels  39.8 us (47%)
  starting transfers between devices  23.4 us (28%)
  waiting for transfers between devices  19.3 us (23%)
  between operations  1.19 us (1%)
    pallas_call x35, Pallas kernels, kernel_call(): pl.pallas_call(kernel, name=name, out_shape=outs, in_specs=specs, out_spe...  39.8 us
    ppermute x12, waiting for transfers between devices, swap(): return lax.ppermute(x, 'tok', partner_pairs(n_tok, stride))  13.1 us
    ppermute x12, starting transfers between devices, swap(): return lax.ppermute(x, 'tok', partner_pairs(n_tok, stride))  11.7 us
    ppermute x5, starting transfers between devices, rotated(): lax.ppermute(x, 'ch', [((i + k) % n_ch, i) for i in range(n_ch)])  7.27 us
    ppermute x3, starting transfers between devices, local(): lax.ppermute(shared if c else late.own, ('tok', 'ch'), pairs)  3.55 us
    ppermute x3, waiting for transfers between devices, local(): lax.ppermute(shared if c else late.own, ('tok', 'ch'), pairs)  2.78 us
    ppermute x5, waiting for transfers between devices, rotated(): lax.ppermute(x, 'ch', [((i + k) % n_ch, i) for i in range(n_ch)])  2.41 us
  transfers between devices with their start and end apart: 21, of which 10 were waited for; matrix products, arithmetic and copies ran while one was open for 0% of the time, Pallas kernels for 29%

profile of v1, /device:TPU:0, one launch (start us, length us, event | category | flops | bytes accessed | tf_op | source)
XLA Modules:
  0.0 83.9 jit_solution(7186437372780025184)
XLA Ops:
  0.6 3.0 %collective-permute-start.1 = (bf16[128,384]{1,0:T(8,128)(2,1)}, bf16[128,384]{1,0:T(8,128)(2,1)S(1)}, u32[]{:S(2)}, u32[]{:S(2)}) collective-permute-start(bf16[128,384]{1,0:T(8,128)(2,1)} %refs_1_.1), channel_id=1, source_target_pairs={{1,0},{0,1},{3,2},{2,3},{5,4},{4,5},{7,6},{6,7},{9,8},{8,9},{11,10... | collective-permute-start | bytes 294920 | tf_op jit(solution)/shard_map/ppermute | solution.py:864
  4.7 1.5 %fetch_kernel.1 = (bf16[384,1536]{1,0:T(8,128)(2,1)S(1)}, bf16[128,384]{1,0:T(8,128)(2,1)S(1)}, f32[384]{0:T(512)S(1)}, bf16[128,384]{1,0:T(8,128)(2,1)S(1)}) custom-call(bf16[384,1536]{1,0:T(8,128)(2,1)} %refs_0_.1, bf16[128,384]{1,0:T(8,128)(2,1)} %refs_1_.1, f32[384]{0:T(512)} %refs_2_.2, bf16[128,384]{1,0:T(8,128)(2,1)} %refs_3_.1, ...), custom_call_target="tpu_custom_call" | custom-call | flops 200000000 | bytes 600000 | tf_op jit(solution)/shard_map/fetch_kernel/pallas_call | solution.py:849
  6.3 2.1 %collective-permute-start = (bf16[128,384]{1,0:T(8,128)(2,1)S(1)}, bf16[128,384]{1,0:T(8,128)(2,1)S(1)}, u32[]{:S(2)}, u32[]{:S(2)}) collective-permute-start(bf16[128,384]{1,0:T(8,128)(2,1)S(1)} %get-tuple-element.127.refs_0_.cot_ref), channel_id=1, source_target_pairs={{1,0},{0,1},{3,2},{2,3},{5,4},{4,5},{7,6},{6,7},{9,8},{8,9},{11,10... | collective-permute-start | bytes 294920 | tf_op jit(solution)/shard_map/ppermute | solution.py:864
  10.7 2.5 %front_kernel.1 = (f32[2,256,128]{2,1,0:T(8,128)S(1)}, f32[3,256,128]{2,1,0:T(8,128)S(1)}, f32[3,256,128]{2,1,0:T(8,128)S(1)}, f32[3,256,128]{2,1,0:T(8,128)S(1)}, f32[3,256,128]{2,1,0:T(8,128)S(1)}) custom-call(bf16[160,384]{1,0:T(8,128)(2,1)S(1)} %collective-permute-done.2.refs_0_, bf16[2,256,384]{2,1,0:T(8,128)(2,1)S(1)} %get-tuple-element.131.sigs_ref.refs_1_.refs_7_, ...), custom_call_target="tpu_custom_call" | custom-call | flops 10000000 | bytes 30000 | tf_op jit(solution)/shard_map/front_kernel/pallas_call | solution.py:849
  13.9 5.6 %forward_kernel_1.1 = (f32[3,256,128]{2,1,0:T(8,128)S(1)}, f32[3,16,8,128]{3,2,1,0:T(8,128)S(1)}, f32[256,2048]{1,0:T(8,128)S(1)}, f32[256,2048]{1,0:T(8,128)S(1...) custom-call(f32[3,256,128]{2,1,0:T(8,128)S(1)} %get-tuple-element.136.gy_ref.refs_0_, ...), custom_call_target="tpu_custom_call" | custom-call | flops 10000000 | bytes 30000 | tf_op jit(solution)/shard_map/forward_kernel_1/pallas_call | solution.py:849
  19.5 5.4 %forward_kernel_0.1 = (f32[3,256,128]{2,1,0:T(8,128)S(1)}, f32[3,16,8,128]{3,2,1,0:T(8,128)S(1)}, f32[256,2048]{1,0:T(8,128)S(1)}, f32[256,2048]{1,0:T(8,128)S(1...) custom-call(f32[3,256,128]{2,1,0:T(8,128)S(1)} %get-tuple-element.136.gy_ref.refs_0_, ...), custom_call_target="tpu_custom_call" | custom-call | flops 10000000 | bytes 30000 | tf_op jit(solution)/shard_map/forward_kernel_0/pallas_call | solution.py:849
  26.0 1.9 %backward_kernel_00.1 = (f32[256,128]{1,0:T(8,128)S(1)}, bf16[256,2048]{1,0:T(8,128)(2,1)S(1)}, f32[256,128]{1,0:T(8,128)S(1)}, f32[24,128]{1,0:T(8,128)S(1)}, f...) custom-call(f32[3,256,128]{2,1,0:T(8,128)S(1)} %get-tuple-element.136.gy_ref.refs_0_, ...), custom_call_target="tpu_custom_call" | custom-call | flops 5000000 | bytes 15000 | tf_op jit(solution)/shard_map/backward_kernel_00/pallas_call | solution.py:849
  27.9 1.5 %collective-permute-start.5 = (bf16[192,384]{1,0:T(8,128)(2,1)S(1)}, bf16[192,384]{1,0:T(8,128)(2,1)S(1)}, u32[]{:S(2)}, u32[]{:S(2)}) collective-permute-start(bf16[192,384]{1,0:T(8,128)(2,1)S(1)} %get-tuple-element.175), channel_id=1, source_target_pairs={{0,4},{2,6},{4,0},{6,2},{8,12},{10,14},{12,8},{14,10},{16,20},{18,... | collective-permute-start | bytes 442376 | tf_op jit(solution)/shard_map/ppermute | solution.py:879
  29.5 2.0 %backward_kernel_01.1 = (f32[256,128]{1,0:T(8,128)S(1)}, bf16[256,2048]{1,0:T(8,128)(2,1)S(1)}, f32[256,128]{1,0:T(8,128)S(1)}, f32[24,128]{1,0:T(8,128)S(1)}, f...) custom-call(f32[3,256,128]{2,1,0:T(8,128)S(1)} %get-tuple-element.136.gy_ref.refs_0_, ...), custom_call_target="tpu_custom_call" | custom-call | flops 5000000 | bytes 15000 | tf_op jit(solution)/shard_map/backward_kernel_01/pallas_call | solution.py:849
  31.4 2.3 %backward_kernel_02.1 = (f32[256,128]{1,0:T(8,128)S(1)}, bf16[256,128]{1,0:T(8,128)(2,1)S(1)}, f32[256,128]{1,0:T(8,128)S(1)}, f32[24,128]{1,0:T(8,128)S(1)}, f3...) custom-call(f32[3,256,128]{2,1,0:T(8,128)S(1)} %get-tuple-element.136.gy_ref.refs_0_, ...), custom_call_target="tpu_custom_call" | custom-call | flops 5000000 | bytes 15000 | tf_op jit(solution)/shard_map/backward_kernel_02/pallas_call | solution.py:849
  34.3 1.6 %collective-permute-start.6 = (bf16[192,384]{1,0:T(8,128)(2,1)S(1)}, bf16[192,384]{1,0:T(8,128)(2,1)S(1)}, u32[]{:S(2)}, u32[]{:S(2)}) collective-permute-start(bf16[192,384]{1,0:T(8,128)(2,1)S(1)} %get-tuple-element.182), channel_id=1, source_target_pairs={{0,8},{2,10},{4,12},{6,14},{8,0},{10,2},{12,4},{14,6},{16,24},{18,... | collective-permute-start | bytes 442376 | tf_op jit(solution)/shard_map/ppermute | solution.py:879
  35.9 1.9 %backward_kernel_10.1 = (f32[256,128]{1,0:T(8,128)S(1)}, bf16[256,2048]{1,0:T(8,128)(2,1)S(1)}, f32[256,128]{1,0:T(8,128)S(1)}, f32[24,128]{1,0:T(8,128)S(1)}, f...) custom-call(f32[3,256,128]{2,1,0:T(8,128)S(1)} %get-tuple-element.136.gy_ref.refs_0_, ...), custom_call_target="tpu_custom_call" | custom-call | flops 5000000 | bytes 15000 | tf_op jit(solution)/shard_map/backward_kernel_10/pallas_call | solution.py:849
  37.8 2.1 %backward_kernel_11.1 = (f32[256,128]{1,0:T(8,128)S(1)}, bf16[256,2048]{1,0:T(8,128)(2,1)S(1)}, f32[256,128]{1,0:T(8,128)S(1)}, f32[24,128]{1,0:T(8,128)S(1)}, f...) custom-call(f32[3,256,128]{2,1,0:T(8,128)S(1)} %get-tuple-element.136.gy_ref.refs_0_, ...), custom_call_target="tpu_custom_call" | custom-call | flops 5000000 | bytes 15000 | tf_op jit(solution)/shard_map/backward_kernel_11/pallas_call | solution.py:849
  40.0 2.7 %collective-permute-start.8 = (bf16[192,384]{1,0:T(8,128)(2,1)S(1)}, bf16[192,384]{1,0:T(8,128)(2,1)S(1)}, u32[]{:S(2)}, u32[]{:S(2)}) collective-permute-start(bf16[192,384]{1,0:T(8,128)(2,1)S(1)} %get-tuple-element.194), channel_id=1, source_target_pairs={{0,16},{2,18},{4,20},{6,22},{8,24},{10,26},{12,28},{14,30},{16,0},... | collective-permute-start | bytes 442376 | tf_op jit(solution)/shard_map/ppermute | solution.py:879
  43.9 2.4 %backward_kernel_12.1 = (f32[256,128]{1,0:T(8,128)S(1)}, bf16[256,128]{1,0:T(8,128)(2,1)S(1)}, f32[256,128]{1,0:T(8,128)S(1)}, f32[24,128]{1,0:T(8,128)S(1)}, f3...) custom-call(f32[3,256,128]{2,1,0:T(8,128)S(1)} %get-tuple-element.136.gy_ref.refs_0_, ...), custom_call_target="tpu_custom_call" | custom-call | flops 5000000 | bytes 15000 | tf_op jit(solution)/shard_map/backward_kernel_12/pallas_call | solution.py:849
  48.6 2.0 %collective-permute-done.7.refs_1_ = bf16[256,128]{1,0:T(8,128)(2,1)S(1)} collective-permute-done((bf16[256,128]{1,0:T(8,128)(2,1)S(1)}, bf16[256,128]{1,0:T(8,128)(2,1)S(1)}, u32[]{:S(2)}, u32[]{:S(2)}) %collective-permute-start.7) | collective-permute-done | bytes 65568 | tf_op jit(solution)/shard_map/ppermute | solution.py:864
  50.7 1.5 %second_conv_kernel.1 = (bf16[256,384]{1,0:T(8,128)(2,1)S(1)}, f32[2,160,384]{2,1,0:T(8,128)S(1)}, bf16[2,160,384]{2,1,0:T(8,128)(2,1)S(1)}) custom-call(s32[256,128]{1,0:T(8,128)S(1)} %get-tuple-element.132.pos_ref.refs_2_.place_ref, s32[256,128]{1,0:T(8,128)S(1)} %get-tuple-element.133.rem_ref.refs_3_.place_ref, ...), custom_call_target="tpu_custom_call" | custom-call | flops 5000000 | bytes 15000 | tf_op jit(solution)/shard_map/second_conv_kernel/pallas_call | solution.py:849
  54.0 1.6 %collective-permute-start.11 = (bf16[160,384]{1,0:T(8,128)(2,1)S(1)}, bf16[160,384]{1,0:T(8,128)(2,1)S(1)}, u32[]{:S(2)}, u32[]{:S(2)}) collective-permute-start(bf16[160,384]{1,0:T(8,128)(2,1)S(1)} %get-tuple-element.222), channel_id=1, source_target_pairs={{0,4},{2,6},{4,0},{6,2},{8,12},{10,14},{12,8},{14,10},{16,20},{18,... | collective-permute-start | bytes 368648 | tf_op jit(solution)/shard_map/ppermute | solution.py:879
  55.6 3.9 %collective-permute-done.11.got_ref = bf16[160,384]{1,0:T(8,128)(2,1)S(1)} collective-permute-done((bf16[160,384]{1,0:T(8,128)(2,1)S(1)}, bf16[160,384]{1,0:T(8,128)(2,1)S(1)}, u32[]{:S(2)}, u32[]{:S(2)}) %collective-permute-start.11) | collective-permute-done | bytes 122912 | tf_op jit(solution)/shard_map/ppermute | solution.py:879
  59.5 1.5 %collective-permute-start.12 = (bf16[160,384]{1,0:T(8,128)(2,1)S(1)}, bf16[160,384]{1,0:T(8,128)(2,1)S(1)}, u32[]{:S(2)}, u32[]{:S(2)}) collective-permute-start(bf16[160,384]{1,0:T(8,128)(2,1)S(1)} %get-tuple-element.224), channel_id=1, source_target_pairs={{0,8},{2,10},{4,12},{6,14},{8,0},{10,2},{12,4},{14,6},{16,24},{18,... | collective-permute-start | bytes 368648 | tf_op jit(solution)/shard_map/ppermute | solution.py:879
  63.0 1.6 %collective-permute-start.15 = (bf16[288,384]{1,0:T(8,128)(2,1)S(1)}, bf16[288,384]{1,0:T(8,128)(2,1)S(1)}, u32[]{:S(2)}, u32[]{:S(2)}) collective-permute-start(bf16[288,384]{1,0:T(8,128)(2,1)S(1)} %stack_kernel.4.refs_0_), channel_id=1, source_target_pairs={{0,4},{2,6},{4,0},{6,2},{8,12},{10,14},{12,8},{14,10},{16,20},{18,... | collective-permute-start | bytes 663560 | tf_op jit(solution)/shard_map/ppermute | solution.py:879
  65.2 7.6 %collective-permute-done.13.got_ref = bf16[160,384]{1,0:T(8,128)(2,1)S(1)} collective-permute-done((bf16[160,384]{1,0:T(8,128)(2,1)S(1)}, bf16[160,384]{1,0:T(8,128)(2,1)S(1)}, u32[]{:S(2)}, u32[]{:S(2)}) %collective-permute-start.13) | collective-permute-done | bytes 122912 | tf_op jit(solution)/shard_map/ppermute | solution.py:879
  75.0 1.5 %collective-permute-start.17 = (bf16[160,384]{1,0:T(8,128)(2,1)S(1)}, bf16[160,384]{1,0:T(8,128)(2,1)S(1)}, u32[]{:S(2)}, u32[]{:S(2)}) collective-permute-start(bf16[160,384]{1,0:T(8,128)(2,1)S(1)} %add_kernel.15.refs_2_.base_ref), channel_id=1, source_target_pairs={{4,0},{5,1},{6,2},{7,3},{0,4},{1,5},{2,6},{3,7},{12,8},{13,9},{14,... | collective-permute-start | bytes 368648 | tf_op jit(solution)/shard_map/ppermute | solution.py:1151
  78.0 2.6 %collective-permute-done.14.refs_0_ = bf16[112,384]{1,0:T(8,128)(2,1)S(1)} collective-permute-done((bf16[112,384]{1,0:T(8,128)(2,1)S(1)}, bf16[112,384]{1,0:T(8,128)(2,1)S(1)}, u32[]{:S(2)}, u32[]{:S(2)}) %collective-permute-start.14) | collective-permute-done | bytes 86048 | tf_op jit(solution)/shard_map/ppermute | solution.py:1151
  (67 shorter events, 20.2 us)
Async XLA Ops:
  0.6 7.7 %collective-permute-start.1 = (bf16[128,384]{1,0:T(8,128)(2,1)}, bf16[128,384]{1,0:T(8,128)(2,1)S(1)}, u32[]{:S(2)}, u32[]{:S(2)}) collective-permute-start(bf16[128,384]{1,0:T(8,128)(2,1)} %refs_1_.1), channel_id=1, source_target_pairs={{1,0},{0,1},{3,2},{2,3},{5,4},{4,5},{7,6},{6,7},{9,8},{8,9},{11,10... | collective-permute-start | bytes 294920 | tf_op jit(solution)/shard_map/ppermute | solution.py:864
  4.7 8.6 %copy-start.4 = (bf16[384,384]{1,0:T(8,128)(2,1)S(1)}, bf16[384,384]{1,0:T(8,128)(2,1)}, u32[]{:S(2)}) copy-start(bf16[384,384]{1,0:T(8,128)(2,1)} %wout_ref.1) | copy-start | bytes 884740
  4.7 6.0 %collective-permute-start.2 = (bf16[160,384]{1,0:T(8,128)(2,1)S(1)}, bf16[160,384]{1,0:T(8,128)(2,1)S(1)}, u32[]{:S(2)}, u32[]{:S(2)}) collective-permute-start(bf16[160,384]{1,0:T(8,128)(2,1)S(1)} %weight_kernel.1.refs_4_.pack_ref.refs_8_), channel_id=1, source_target_pairs={{1,0},{0,1},{3,2},{2,3},{5,4},{4,5},{7,6},{6,7},{9,8},{8,9},{11,10... | collective-permute-start | bytes 368648 | tf_op jit(solution)/shard_map/ppermute | solution.py:864
  6.2 7.6 %copy-start = (bf16[2048,128]{1,0:T(8,128)(2,1)S(1)}, bf16[2048,128]{1,0:T(8,128)(2,1)}, u32[]{:S(2)}) copy-start(bf16[2048,128]{1,0:T(8,128)(2,1)} %constant.5.clone.er_ref.refs_13_) | copy-start | bytes 1572868
  6.3 6.9 %collective-permute-start = (bf16[128,384]{1,0:T(8,128)(2,1)S(1)}, bf16[128,384]{1,0:T(8,128)(2,1)S(1)}, u32[]{:S(2)}, u32[]{:S(2)}) collective-permute-start(bf16[128,384]{1,0:T(8,128)(2,1)S(1)} %get-tuple-element.127.refs_0_.cot_ref), channel_id=1, source_target_pairs={{1,0},{0,1},{3,2},{2,3},{5,4},{4,5},{7,6},{6,7},{9,8},{8,9},{11,10... | collective-permute-start | bytes 294920 | tf_op jit(solution)/shard_map/ppermute | solution.py:864
  13.9 11.0 %copy-start.5 = (f32[2,384]{1,0:T(2,128)S(1)}, f32[2,384]{1,0:T(2,128)}, u32[]{:S(2)}) copy-start(f32[2,384]{1,0:T(2,128)} %refs_11_.11) | copy-start | bytes 9220
  25.9 2.0 %collective-permute-start.4 = (bf16[2,192,384]{2,1,0:T(8,128)(2,1)S(1)}, bf16[2,192,384]{2,1,0:T(8,128)(2,1)S(1)}, u32[]{:S(2)}, u32[]{:S(2)}) collective-permute-start(bf16[2,192,384]{2,1,0:T(8,128)(2,1)S(1)} %get-tuple-element.172), channel_id=1, source_target_pairs={{0,2},{2,0},{4,6},{6,4},{8,10},{10,8},{12,14},{14,12},{16,18},{18,... | collective-permute-start | bytes 884744 | tf_op jit(solution)/shard_map/ppermute | solution.py:879
  27.9 6.3 %collective-permute-start.5 = (bf16[192,384]{1,0:T(8,128)(2,1)S(1)}, bf16[192,384]{1,0:T(8,128)(2,1)S(1)}, u32[]{:S(2)}, u32[]{:S(2)}) collective-permute-start(bf16[192,384]{1,0:T(8,128)(2,1)S(1)} %get-tuple-element.175), channel_id=1, source_target_pairs={{0,4},{2,6},{4,0},{6,2},{8,12},{10,14},{12,8},{14,10},{16,20},{18,... | collective-permute-start | bytes 442376 | tf_op jit(solution)/shard_map/ppermute | solution.py:879
  34.3 5.7 %collective-permute-start.6 = (bf16[192,384]{1,0:T(8,128)(2,1)S(1)}, bf16[192,384]{1,0:T(8,128)(2,1)S(1)}, u32[]{:S(2)}, u32[]{:S(2)}) collective-permute-start(bf16[192,384]{1,0:T(8,128)(2,1)S(1)} %get-tuple-element.182), channel_id=1, source_target_pairs={{0,8},{2,10},{4,12},{6,14},{8,0},{10,2},{12,4},{14,6},{16,24},{18,... | collective-permute-start | bytes 442376 | tf_op jit(solution)/shard_map/ppermute | solution.py:879
  40.0 10.6 %collective-permute-start.8 = (bf16[192,384]{1,0:T(8,128)(2,1)S(1)}, bf16[192,384]{1,0:T(8,128)(2,1)S(1)}, u32[]{:S(2)}, u32[]{:S(2)}) collective-permute-start(bf16[192,384]{1,0:T(8,128)(2,1)S(1)} %get-tuple-element.194), channel_id=1, source_target_pairs={{0,16},{2,18},{4,20},{6,22},{8,24},{10,26},{12,28},{14,30},{16,0},... | collective-permute-start | bytes 442376 | tf_op jit(solution)/shard_map/ppermute | solution.py:879
  42.7 4.5 %collective-permute-start.3 = (bf16[256,128]{1,0:T(8,128)(2,1)S(1)}, bf16[256,128]{1,0:T(8,128)(2,1)S(1)}, u32[]{:S(2)}, u32[]{:S(2)}) collective-permute-start(bf16[256,128]{1,0:T(8,128)(2,1)S(1)} %get-tuple-element.159), channel_id=1, source_target_pairs={{1,0},{0,1},{3,2},{2,3},{5,4},{4,5},{7,6},{6,7},{9,8},{8,9},{11,10... | collective-permute-start | bytes 196616 | tf_op jit(solution)/shard_map/ppermute | solution.py:864
  46.3 4.3 %collective-permute-start.7 = (bf16[256,128]{1,0:T(8,128)(2,1)S(1)}, bf16[256,128]{1,0:T(8,128)(2,1)S(1)}, u32[]{:S(2)}, u32[]{:S(2)}) collective-permute-start(bf16[256,128]{1,0:T(8,128)(2,1)S(1)} %get-tuple-element.189), channel_id=1, source_target_pairs={{1,0},{0,1},{3,2},{2,3},{5,4},{4,5},{7,6},{6,7},{9,8},{8,9},{11,10... | collective-permute-start | bytes 196616 | tf_op jit(solution)/shard_map/ppermute | solution.py:864
  52.2 1.8 %collective-permute-start.10 = (bf16[2,160,384]{2,1,0:T(8,128)(2,1)S(1)}, bf16[2,160,384]{2,1,0:T(8,128)(2,1)S(1)}, u32[]{:S(2)}, u32[]{:S(2)}) collective-permute-start(bf16[2,160,384]{2,1,0:T(8,128)(2,1)S(1)} %get-tuple-element.220), channel_id=1, source_target_pairs={{0,2},{2,0},{4,6},{6,4},{8,10},{10,8},{12,14},{14,12},{16,18},{18,... | collective-permute-start | bytes 737288 | tf_op jit(solution)/shard_map/ppermute | solution.py:879
  53.1 8.9 %collective-permute-start.9 = (bf16[352,384]{1,0:T(8,128)(2,1)S(1)}, bf16[352,384]{1,0:T(8,128)(2,1)S(1)}, u32[]{:S(2)}, u32[]{:S(2)}) collective-permute-start(bf16[352,384]{1,0:T(8,128)(2,1)S(1)} %stack_kernel.3), channel_id=1, source_target_pairs={{0,1},{1,0},{2,3},{3,2},{4,5},{5,4},{6,7},{7,6},{8,9},{9,8},{10,11... | collective-permute-start | bytes 811016 | tf_op jit(solution)/shard_map/ppermute | solution.py:870
  54.0 5.5 %collective-permute-start.11 = (bf16[160,384]{1,0:T(8,128)(2,1)S(1)}, bf16[160,384]{1,0:T(8,128)(2,1)S(1)}, u32[]{:S(2)}, u32[]{:S(2)}) collective-permute-start(bf16[160,384]{1,0:T(8,128)(2,1)S(1)} %get-tuple-element.222), channel_id=1, source_target_pairs={{0,4},{2,6},{4,0},{6,2},{8,12},{10,14},{12,8},{14,10},{16,20},{18,... | collective-permute-start | bytes 368648 | tf_op jit(solution)/shard_map/ppermute | solution.py:879
  59.5 5.0 %collective-permute-start.12 = (bf16[160,384]{1,0:T(8,128)(2,1)S(1)}, bf16[160,384]{1,0:T(8,128)(2,1)S(1)}, u32[]{:S(2)}, u32[]{:S(2)}) collective-permute-start(bf16[160,384]{1,0:T(8,128)(2,1)S(1)} %get-tuple-element.224), channel_id=1, source_target_pairs={{0,8},{2,10},{4,12},{6,14},{8,0},{10,2},{12,4},{14,6},{16,24},{18,... | collective-permute-start | bytes 368648 | tf_op jit(solution)/shard_map/ppermute | solution.py:879
  63.0 9.9 %collective-permute-start.15 = (bf16[288,384]{1,0:T(8,128)(2,1)S(1)}, bf16[288,384]{1,0:T(8,128)(2,1)S(1)}, u32[]{:S(2)}, u32[]{:S(2)}) collective-permute-start(bf16[288,384]{1,0:T(8,128)(2,1)S(1)} %stack_kernel.4.refs_0_), channel_id=1, source_target_pairs={{0,4},{2,6},{4,0},{6,2},{8,12},{10,14},{12,8},{14,10},{16,20},{18,... | collective-permute-start | bytes 663560 | tf_op jit(solution)/shard_map/ppermute | solution.py:879
  64.6 8.3 %collective-permute-start.13 = (bf16[160,384]{1,0:T(8,128)(2,1)S(1)}, bf16[160,384]{1,0:T(8,128)(2,1)S(1)}, u32[]{:S(2)}, u32[]{:S(2)}) collective-permute-start(bf16[160,384]{1,0:T(8,128)(2,1)S(1)} %get-tuple-element.227), channel_id=1, source_target_pairs={{0,16},{2,18},{4,20},{6,22},{8,24},{10,26},{12,28},{14,30},{16,0},... | collective-permute-start | bytes 368648 | tf_op jit(solution)/shard_map/ppermute | solution.py:879
  72.9 3.7 %collective-permute-start.16 = (bf16[2,288,384]{2,1,0:T(8,128)(2,1)S(1)}, bf16[2,288,384]{2,1,0:T(8,128)(2,1)S(1)}, u32[]{:S(2)}, u32[]{:S(2)}) collective-permute-start(bf16[2,288,384]{2,1,0:T(8,128)(2,1)S(1)} %bitcast.3), channel_id=1, source_target_pairs={{0,2},{2,0},{4,6},{6,4},{8,10},{10,8},{12,14},{14,12},{16,18},{18,... | collective-permute-start | bytes 1327112 | tf_op jit(solution)/shard_map/ppermute | solution.py:879
  73.0 7.7 %collective-permute-start.18 = (bf16[112,384]{1,0:T(8,128)(2,1)S(1)}, bf16[112,384]{1,0:T(8,128)(2,1)S(1)}, u32[]{:S(2)}, u32[]{:S(2)}) collective-permute-start(bf16[112,384]{1,0:T(8,128)(2,1)S(1)} %slice.4), channel_id=1, source_target_pairs={{5,0},{4,1},{7,2},{6,3},{1,4},{0,5},{3,6},{2,7},{13,8},{12,9},{15,... | collective-permute-start | bytes 258056 | tf_op jit(solution)/shard_map/ppermute | solution.py:1151
  74.1 6.5 %collective-permute-start.14 = (bf16[112,384]{1,0:T(8,128)(2,1)S(1)}, bf16[112,384]{1,0:T(8,128)(2,1)S(1)}, u32[]{:S(2)}, u32[]{:S(2)}) collective-permute-start(bf16[112,384]{1,0:T(8,128)(2,1)S(1)} %slice.4), channel_id=1, source_target_pairs={{1,0},{0,1},{3,2},{2,3},{5,4},{4,5},{7,6},{6,7},{9,8},{8,9},{11,10... | collective-permute-start | bytes 258056 | tf_op jit(solution)/shard_map/ppermute | solution.py:1151
  75.0 5.8 %collective-permute-start.17 = (bf16[160,384]{1,0:T(8,128)(2,1)S(1)}, bf16[160,384]{1,0:T(8,128)(2,1)S(1)}, u32[]{:S(2)}, u32[]{:S(2)}) collective-permute-start(bf16[160,384]{1,0:T(8,128)(2,1)S(1)} %add_kernel.15.refs_2_.base_ref), channel_id=1, source_target_pairs={{4,0},{5,1},{6,2},{7,3},{0,4},{1,5},{2,6},{3,7},{12,8},{13,9},{14,... | collective-permute-start | bytes 368648 | tf_op jit(solution)/shard_map/ppermute | solution.py:1151
  80.6 1.5 %collective-permute-start.19 = (bf16[256,384]{1,0:T(8,128)(2,1)S(1)}, bf16[256,384]{1,0:T(8,128)(2,1)S(1)}, u32[]{:S(2)}, u32[]{:S(2)}) collective-permute-start(bf16[256,384]{1,0:T(8,128)(2,1)S(1)} %join_kernel.2.refs_0_), channel_id=1, source_target_pairs={{0,2},{2,0},{4,6},{6,4},{8,10},{10,8},{12,14},{14,12},{16,18},{18,... | collective-permute-start | bytes 589832 | tf_op jit(solution)/shard_map/ppermute | solution.py:879
  80.9 1.5 %collective-permute-start.20 = (bf16[256,384]{1,0:T(8,128)(2,1)S(1)}, bf16[256,384]{1,0:T(8,128)(2,1)S(1)}, u32[]{:S(2)}, u32[]{:S(2)}) collective-permute-start(bf16[256,384]{1,0:T(8,128)(2,1)S(1)} %join_kernel.3.refs_1_), channel_id=1, source_target_pairs={{0,2},{2,0},{4,6},{6,4},{8,10},{10,8},{12,14},{14,12},{16,18},{18,... | collective-permute-start | bytes 589832 | tf_op jit(solution)/shard_map/ppermute | solution.py:879
  (3 other events, 21.7 us)

commit v2 on v1

--- a/solution.py
+++ b/solution.py
@@ -16,10 +16,9 @@
 HUGE_STEP = 1e30
 LOG2E = math.log2(math.e)
 LN2 = math.log(2.0)
-BLOCK = 64
+BLOCK = 128
 PAIRS = 8
 PIECES = 4
-FETCHES = 8
 
 
 def mm(a, b):
@@ -163,13 +162,11 @@
         packed_ref[:, real:] = jnp.zeros((LANES + 32, packed_ref.shape[1] - real), LOW)
 
 
-def fetch_kernel(n, *refs):
-    sources, targets, sems = refs[:n], refs[n + 1:2 * n + 1], refs[-1]
-    rows = sources[0].shape[0] // FETCHES
-    parts = [pl.ds(i * rows, rows) for i in range(FETCHES)]
+def fetch_kernel(inner, chans, win_hbm, own_hbm, gain_hbm, cot_hbm, _, win_ref, own_ref, gain_ref, cot_ref, sems):
+    first = pl.multiple_of(inner + lax.axis_index("ch") * chans, LANES)
     for copy in fetch_all(
-        [sources[0].at[part, :] for part in parts] + list(sources[1:]),
-        [targets[0].at[part, :] for part in parts] + list(targets[1:]), sems,
+        (win_hbm.at[:, 0:inner], win_hbm.at[:, pl.ds(first, chans)], own_hbm, gain_hbm, cot_hbm),
+        (win_ref.at[:, 0:inner], win_ref.at[:, inner:inner + chans], own_ref, gain_ref, cot_ref), sems,
     ):
         copy.wait()
 
@@ -196,7 +193,7 @@
         j = lax.rem(me + k, n_ch)
         sigs_ref[k] = mm(normed, win_ref[:, pl.ds(pl.multiple_of(j * chans, LANES), chans)]).astype(LOW)
     gate_ref[...] = mm(
-        normed, win_ref[:, pl.ds(pl.multiple_of(inner + me * chans, LANES), chans)]
+        normed, win_ref[:, inner:inner + chans]
     ).astype(LOW)
     fetch.wait()
     pos, rem = clip_places(len_ref, total, (total, LANES))
@@ -709,7 +706,7 @@
 def grad_normed(dims, me, gsig, ggate_ref, win_ref):
     n_ch, n_tok, rows, width, chans, inner, rank, states, taps = dims
     return mm_nt(gsig, win_ref[:, pl.ds(pl.multiple_of(me * chans, LANES), chans)]) + mm_nt(
-        ggate_ref[...], win_ref[:, pl.ds(pl.multiple_of(inner + me * chans, LANES), chans)]
+        ggate_ref[...], win_ref[:, inner:inner + chans]
     )
 
 
@@ -999,8 +996,8 @@
     pack_parts = rotated(packed, n_ch)
     fetched = (in_proj, tokens, norm_gain, cotangent)
     win, own, gain, cot_own = kernel_call(
-        functools.partial(fetch_kernel, len(fetched)), "fetch_kernel", (*far(*fetched), packed),
-        [shape(x.shape, x.dtype) for x in fetched], [dma((FETCHES + len(fetched) - 1,))], limit, 20,
+        functools.partial(fetch_kernel, inner, chans), "fetch_kernel", (*far(*fetched), packed),
+        [shape((width, inner + chans), LOW)] + [shape(x.shape, x.dtype) for x in fetched[1:]], [dma((5,))], limit, 20,
         [(i, pltpu.HBM) for i in range(len(fetched))] + [(len(fetched), pl.ANY)],
     )
     normed, xp, sigs, gate, pos, rem = kernel_call(

time: 84 us -> 84.2 us (level)
  transfers between devices with their start and end apart: 21 -> 21, of which waited for: 10 -> 9; matrix products, arithmetic and copies ran while one was open for 0% -> 0% of each run, Pallas kernels for 29% -> 28%
where the time goes in v2:
time: 84.2 us; the launch traced here: 84 us
  Pallas kernels  39.4 us (47%)
  starting transfers between devices  23.6 us (28%)
  waiting for transfers between devices  19.7 us (23%)
  between operations  1.2 us (1%)
    pallas_call x35, Pallas kernels, kernel_call(): pl.pallas_call(kernel, name=name, out_shape=outs, in_specs=specs, out_spe...  39.4 us
    ppermute x12, waiting for transfers between devices, swap(): return lax.ppermute(x, 'tok', partner_pairs(n_tok, stride))  13.1 us
    ppermute x12, starting transfers between devices, swap(): return lax.ppermute(x, 'tok', partner_pairs(n_tok, stride))  12.1 us
    ppermute x5, starting transfers between devices, rotated(): lax.ppermute(x, 'ch', [((i + k) % n_ch, i) for i in range(n_ch)])  7.28 us
    ppermute x3, starting transfers between devices, local(): lax.ppermute(shared if c else late.own, ('tok', 'ch'), pairs)  3.55 us
    ppermute x5, waiting for transfers between devices, rotated(): lax.ppermute(x, 'ch', [((i + k) % n_ch, i) for i in range(n_ch)])  2.86 us
    ppermute x3, waiting for transfers between devices, local(): lax.ppermute(shared if c else late.own, ('tok', 'ch'), pairs)  2.65 us
  transfers between devices with their start and end apart: 21, of which 9 were waited for; matrix products, arithmetic and copies ran while one was open for 0% of the time, Pallas kernels for 28%

profile of v2, /device:TPU:0, one launch (start us, length us, event | category | flops | bytes accessed | tf_op | source)
XLA Modules:
  0.0 84.0 jit_solution(2669986007572797444)
XLA Ops:
  0.6 3.0 %collective-permute-start.1 = (bf16[128,384]{1,0:T(8,128)(2,1)}, bf16[128,384]{1,0:T(8,128)(2,1)S(1)}, u32[]{:S(2)}, u32[]{:S(2)}) collective-permute-start(bf16[128,384]{1,0:T(8,128)(2,1)} %own_hbm.1), channel_id=1, source_target_pairs={{1,0},{0,1},{3,2},{2,3},{5,4},{4,5},{7,6},{6,7},{9,8},{8,9},{11,10... | collective-permute-start | bytes 294920 | tf_op jit(solution)/shard_map/ppermute | solution.py:861
  6.0 2.1 %collective-permute-start = (bf16[128,384]{1,0:T(8,128)(2,1)S(1)}, bf16[128,384]{1,0:T(8,128)(2,1)S(1)}, u32[]{:S(2)}, u32[]{:S(2)}) collective-permute-start(bf16[128,384]{1,0:T(8,128)(2,1)S(1)} %get-tuple-element.127.refs_0_.cot_ref), channel_id=1, source_target_pairs={{1,0},{0,1},{3,2},{2,3},{5,4},{4,5},{7,6},{6,7},{9,8},{8,9},{11,10... | collective-permute-start | bytes 294920 | tf_op jit(solution)/shard_map/ppermute | solution.py:861
  10.6 2.5 %front_kernel.1 = (f32[2,256,128]{2,1,0:T(8,128)S(1)}, f32[3,256,128]{2,1,0:T(8,128)S(1)}, f32[3,256,128]{2,1,0:T(8,128)S(1)}, f32[3,256,128]{2,1,0:T(8,128)S(1)}, f32[3,256,128]{2,1,0:T(8,128)S(1)}) custom-call(bf16[160,384]{1,0:T(8,128)(2,1)S(1)} %collective-permute-done.2.refs_0_, bf16[2,256,384]{2,1,0:T(8,128)(2,1)S(1)} %get-tuple-element.131.sigs_ref.refs_1_.refs_7_, ...), custom_call_target="tpu_custom_call" | custom-call | flops 10000000 | bytes 30000 | tf_op jit(solution)/shard_map/front_kernel/pallas_call | solution.py:846
  13.8 5.6 %forward_kernel_1.1 = (f32[3,256,128]{2,1,0:T(8,128)S(1)}, f32[3,16,8,128]{3,2,1,0:T(8,128)S(1)}, f32[256,2048]{1,0:T(8,128)S(1)}, f32[256,2048]{1,0:T(8,128)S(1...) custom-call(f32[3,256,128]{2,1,0:T(8,128)S(1)} %get-tuple-element.136.gy_ref.refs_0_, ...), custom_call_target="tpu_custom_call" | custom-call | flops 10000000 | bytes 30000 | tf_op jit(solution)/shard_map/forward_kernel_1/pallas_call | solution.py:846
  19.4 5.4 %forward_kernel_0.1 = (f32[3,256,128]{2,1,0:T(8,128)S(1)}, f32[3,16,8,128]{3,2,1,0:T(8,128)S(1)}, f32[256,2048]{1,0:T(8,128)S(1)}, f32[256,2048]{1,0:T(8,128)S(1...) custom-call(f32[3,256,128]{2,1,0:T(8,128)S(1)} %get-tuple-element.136.gy_ref.refs_0_, ...), custom_call_target="tpu_custom_call" | custom-call | flops 10000000 | bytes 30000 | tf_op jit(solution)/shard_map/forward_kernel_0/pallas_call | solution.py:846
  25.9 1.9 %backward_kernel_00.1 = (f32[256,128]{1,0:T(8,128)S(1)}, bf16[256,2048]{1,0:T(8,128)(2,1)S(1)}, f32[256,128]{1,0:T(8,128)S(1)}, f32[24,128]{1,0:T(8,128)S(1)}, f...) custom-call(f32[3,256,128]{2,1,0:T(8,128)S(1)} %get-tuple-element.136.gy_ref.refs_0_, ...), custom_call_target="tpu_custom_call" | custom-call | flops 5000000 | bytes 15000 | tf_op jit(solution)/shard_map/backward_kernel_00/pallas_call | solution.py:846
  27.8 1.6 %collective-permute-start.5 = (bf16[192,384]{1,0:T(8,128)(2,1)S(1)}, bf16[192,384]{1,0:T(8,128)(2,1)S(1)}, u32[]{:S(2)}, u32[]{:S(2)}) collective-permute-start(bf16[192,384]{1,0:T(8,128)(2,1)S(1)} %get-tuple-element.175), channel_id=1, source_target_pairs={{0,4},{2,6},{4,0},{6,2},{8,12},{10,14},{12,8},{14,10},{16,20},{18,... | collective-permute-start | bytes 442376 | tf_op jit(solution)/shard_map/ppermute | solution.py:876
  29.4 2.0 %backward_kernel_01.1 = (f32[256,128]{1,0:T(8,128)S(1)}, bf16[256,2048]{1,0:T(8,128)(2,1)S(1)}, f32[256,128]{1,0:T(8,128)S(1)}, f32[24,128]{1,0:T(8,128)S(1)}, f...) custom-call(f32[3,256,128]{2,1,0:T(8,128)S(1)} %get-tuple-element.136.gy_ref.refs_0_, ...), custom_call_target="tpu_custom_call" | custom-call | flops 5000000 | bytes 15000 | tf_op jit(solution)/shard_map/backward_kernel_01/pallas_call | solution.py:846
  31.4 2.3 %backward_kernel_02.1 = (f32[256,128]{1,0:T(8,128)S(1)}, bf16[256,128]{1,0:T(8,128)(2,1)S(1)}, f32[256,128]{1,0:T(8,128)S(1)}, f32[24,128]{1,0:T(8,128)S(1)}, f3...) custom-call(f32[3,256,128]{2,1,0:T(8,128)S(1)} %get-tuple-element.136.gy_ref.refs_0_, ...), custom_call_target="tpu_custom_call" | custom-call | flops 5000000 | bytes 15000 | tf_op jit(solution)/shard_map/backward_kernel_02/pallas_call | solution.py:846
  34.2 1.7 %collective-permute-start.6 = (bf16[192,384]{1,0:T(8,128)(2,1)S(1)}, bf16[192,384]{1,0:T(8,128)(2,1)S(1)}, u32[]{:S(2)}, u32[]{:S(2)}) collective-permute-start(bf16[192,384]{1,0:T(8,128)(2,1)S(1)} %get-tuple-element.182), channel_id=1, source_target_pairs={{0,8},{2,10},{4,12},{6,14},{8,0},{10,2},{12,4},{14,6},{16,24},{18,... | collective-permute-start | bytes 442376 | tf_op jit(solution)/shard_map/ppermute | solution.py:876
  35.9 1.9 %backward_kernel_10.1 = (f32[256,128]{1,0:T(8,128)S(1)}, bf16[256,2048]{1,0:T(8,128)(2,1)S(1)}, f32[256,128]{1,0:T(8,128)S(1)}, f32[24,128]{1,0:T(8,128)S(1)}, f...) custom-call(f32[3,256,128]{2,1,0:T(8,128)S(1)} %get-tuple-element.136.gy_ref.refs_0_, ...), custom_call_target="tpu_custom_call" | custom-call | flops 5000000 | bytes 15000 | tf_op jit(solution)/shard_map/backward_kernel_10/pallas_call | solution.py:846
  37.8 2.1 %backward_kernel_11.1 = (f32[256,128]{1,0:T(8,128)S(1)}, bf16[256,2048]{1,0:T(8,128)(2,1)S(1)}, f32[256,128]{1,0:T(8,128)S(1)}, f32[24,128]{1,0:T(8,128)S(1)}, f...) custom-call(f32[3,256,128]{2,1,0:T(8,128)S(1)} %get-tuple-element.136.gy_ref.refs_0_, ...), custom_call_target="tpu_custom_call" | custom-call | flops 5000000 | bytes 15000 | tf_op jit(solution)/shard_map/backward_kernel_11/pallas_call | solution.py:846
  40.0 2.6 %collective-permute-start.8 = (bf16[192,384]{1,0:T(8,128)(2,1)S(1)}, bf16[192,384]{1,0:T(8,128)(2,1)S(1)}, u32[]{:S(2)}, u32[]{:S(2)}) collective-permute-start(bf16[192,384]{1,0:T(8,128)(2,1)S(1)} %get-tuple-element.194), channel_id=1, source_target_pairs={{0,16},{2,18},{4,20},{6,22},{8,24},{10,26},{12,28},{14,30},{16,0},... | collective-permute-start | bytes 442376 | tf_op jit(solution)/shard_map/ppermute | solution.py:876
  42.6 1.4 %collective-permute-start.3 = (bf16[256,128]{1,0:T(8,128)(2,1)S(1)}, bf16[256,128]{1,0:T(8,128)(2,1)S(1)}, u32[]{:S(2)}, u32[]{:S(2)}) collective-permute-start(bf16[256,128]{1,0:T(8,128)(2,1)S(1)} %get-tuple-element.159), channel_id=1, source_target_pairs={{1,0},{0,1},{3,2},{2,3},{5,4},{4,5},{7,6},{6,7},{9,8},{8,9},{11,10... | collective-permute-start | bytes 196616 | tf_op jit(solution)/shard_map/ppermute | solution.py:861
  44.0 2.4 %backward_kernel_12.1 = (f32[256,128]{1,0:T(8,128)S(1)}, bf16[256,128]{1,0:T(8,128)(2,1)S(1)}, f32[256,128]{1,0:T(8,128)S(1)}, f32[24,128]{1,0:T(8,128)S(1)}, f3...) custom-call(f32[3,256,128]{2,1,0:T(8,128)S(1)} %get-tuple-element.136.gy_ref.refs_0_, ...), custom_call_target="tpu_custom_call" | custom-call | flops 5000000 | bytes 15000 | tf_op jit(solution)/shard_map/backward_kernel_12/pallas_call | solution.py:846
  48.5 2.3 %collective-permute-done.7.refs_1_ = bf16[256,128]{1,0:T(8,128)(2,1)S(1)} collective-permute-done((bf16[256,128]{1,0:T(8,128)(2,1)S(1)}, bf16[256,128]{1,0:T(8,128)(2,1)S(1)}, u32[]{:S(2)}, u32[]{:S(2)}) %collective-permute-start.7) | collective-permute-done | bytes 65568 | tf_op jit(solution)/shard_map/ppermute | solution.py:861
  50.8 1.5 %second_conv_kernel.1 = (bf16[256,384]{1,0:T(8,128)(2,1)S(1)}, f32[2,160,384]{2,1,0:T(8,128)S(1)}, bf16[2,160,384]{2,1,0:T(8,128)(2,1)S(1)}) custom-call(s32[256,128]{1,0:T(8,128)S(1)} %get-tuple-element.132.pos_ref.refs_2_.place_ref, s32[256,128]{1,0:T(8,128)S(1)} %get-tuple-element.133.rem_ref.refs_3_.place_ref, ...), custom_call_target="tpu_custom_call" | custom-call | flops 5000000 | bytes 15000 | tf_op jit(solution)/shard_map/second_conv_kernel/pallas_call | solution.py:846
  54.0 1.6 %collective-permute-start.11 = (bf16[160,384]{1,0:T(8,128)(2,1)S(1)}, bf16[160,384]{1,0:T(8,128)(2,1)S(1)}, u32[]{:S(2)}, u32[]{:S(2)}) collective-permute-start(bf16[160,384]{1,0:T(8,128)(2,1)S(1)} %get-tuple-element.222), channel_id=1, source_target_pairs={{0,4},{2,6},{4,0},{6,2},{8,12},{10,14},{12,8},{14,10},{16,20},{18,... | collective-permute-start | bytes 368648 | tf_op jit(solution)/shard_map/ppermute | solution.py:876
  55.5 3.9 %collective-permute-done.11.got_ref = bf16[160,384]{1,0:T(8,128)(2,1)S(1)} collective-permute-done((bf16[160,384]{1,0:T(8,128)(2,1)S(1)}, bf16[160,384]{1,0:T(8,128)(2,1)S(1)}, u32[]{:S(2)}, u32[]{:S(2)}) %collective-permute-start.11) | collective-permute-done | bytes 122912 | tf_op jit(solution)/shard_map/ppermute | solution.py:876
  59.5 1.5 %collective-permute-start.12 = (bf16[160,384]{1,0:T(8,128)(2,1)S(1)}, bf16[160,384]{1,0:T(8,128)(2,1)S(1)}, u32[]{:S(2)}, u32[]{:S(2)}) collective-permute-start(bf16[160,384]{1,0:T(8,128)(2,1)S(1)} %get-tuple-element.224), channel_id=1, source_target_pairs={{0,8},{2,10},{4,12},{6,14},{8,0},{10,2},{12,4},{14,6},{16,24},{18,... | collective-permute-start | bytes 368648 | tf_op jit(solution)/shard_map/ppermute | solution.py:876
  63.1 1.6 %collective-permute-start.15 = (bf16[288,384]{1,0:T(8,128)(2,1)S(1)}, bf16[288,384]{1,0:T(8,128)(2,1)S(1)}, u32[]{:S(2)}, u32[]{:S(2)}) collective-permute-start(bf16[288,384]{1,0:T(8,128)(2,1)S(1)} %stack_kernel.4.refs_0_), channel_id=1, source_target_pairs={{0,4},{2,6},{4,0},{6,2},{8,12},{10,14},{12,8},{14,10},{16,20},{18,... | collective-permute-start | bytes 663560 | tf_op jit(solution)/shard_map/ppermute | solution.py:876
  65.4 7.6 %collective-permute-done.13.got_ref = bf16[160,384]{1,0:T(8,128)(2,1)S(1)} collective-permute-done((bf16[160,384]{1,0:T(8,128)(2,1)S(1)}, bf16[160,384]{1,0:T(8,128)(2,1)S(1)}, u32[]{:S(2)}, u32[]{:S(2)}) %collective-permute-start.13) | collective-permute-done | bytes 122912 | tf_op jit(solution)/shard_map/ppermute | solution.py:876
  75.2 1.5 %collective-permute-start.17 = (bf16[160,384]{1,0:T(8,128)(2,1)S(1)}, bf16[160,384]{1,0:T(8,128)(2,1)S(1)}, u32[]{:S(2)}, u32[]{:S(2)}) collective-permute-start(bf16[160,384]{1,0:T(8,128)(2,1)S(1)} %add_kernel.15.refs_2_.base_ref), channel_id=1, source_target_pairs={{4,0},{5,1},{6,2},{7,3},{0,4},{1,5},{2,6},{3,7},{12,8},{13,9},{14,... | collective-permute-start | bytes 368648 | tf_op jit(solution)/shard_map/ppermute | solution.py:1148
  78.1 2.6 %collective-permute-done.14.refs_0_ = bf16[112,384]{1,0:T(8,128)(2,1)S(1)} collective-permute-done((bf16[112,384]{1,0:T(8,128)(2,1)S(1)}, bf16[112,384]{1,0:T(8,128)(2,1)S(1)}, u32[]{:S(2)}, u32[]{:S(2)}) %collective-permute-start.14) | collective-permute-done | bytes 86048 | tf_op jit(solution)/shard_map/ppermute | solution.py:1148
  (67 shorter events, 20.2 us)
Async XLA Ops:
  0.6 7.5 %collective-permute-start.1 = (bf16[128,384]{1,0:T(8,128)(2,1)}, bf16[128,384]{1,0:T(8,128)(2,1)S(1)}, u32[]{:S(2)}, u32[]{:S(2)}) collective-permute-start(bf16[128,384]{1,0:T(8,128)(2,1)} %own_hbm.1), channel_id=1, source_target_pairs={{1,0},{0,1},{3,2},{2,3},{5,4},{4,5},{7,6},{6,7},{9,8},{8,9},{11,10... | collective-permute-start | bytes 294920 | tf_op jit(solution)/shard_map/ppermute | solution.py:861
  4.7 8.5 %copy-start.4 = (bf16[384,384]{1,0:T(8,128)(2,1)S(1)}, bf16[384,384]{1,0:T(8,128)(2,1)}, u32[]{:S(2)}) copy-start(bf16[384,384]{1,0:T(8,128)(2,1)} %wout_ref.1) | copy-start | bytes 884740
  4.7 6.0 %collective-permute-start.2 = (bf16[160,384]{1,0:T(8,128)(2,1)S(1)}, bf16[160,384]{1,0:T(8,128)(2,1)S(1)}, u32[]{:S(2)}, u32[]{:S(2)}) collective-permute-start(bf16[160,384]{1,0:T(8,128)(2,1)S(1)} %weight_kernel.1._.pack_ref.refs_8_), channel_id=1, source_target_pairs={{1,0},{0,1},{3,2},{2,3},{5,4},{4,5},{7,6},{6,7},{9,8},{8,9},{11,10... | collective-permute-start | bytes 368648 | tf_op jit(solution)/shard_map/ppermute | solution.py:861
  6.0 7.8 %copy-start = (bf16[2048,128]{1,0:T(8,128)(2,1)S(1)}, bf16[2048,128]{1,0:T(8,128)(2,1)}, u32[]{:S(2)}) copy-start(bf16[2048,128]{1,0:T(8,128)(2,1)} %constant.5.clone.er_ref.refs_13_) | copy-start | bytes 1572868
  6.0 7.1 %collective-permute-start = (bf16[128,384]{1,0:T(8,128)(2,1)S(1)}, bf16[128,384]{1,0:T(8,128)(2,1)S(1)}, u32[]{:S(2)}, u32[]{:S(2)}) collective-permute-start(bf16[128,384]{1,0:T(8,128)(2,1)S(1)} %get-tuple-element.127.refs_0_.cot_ref), channel_id=1, source_target_pairs={{1,0},{0,1},{3,2},{2,3},{5,4},{4,5},{7,6},{6,7},{9,8},{8,9},{11,10... | collective-permute-start | bytes 294920 | tf_op jit(solution)/shard_map/ppermute | solution.py:861
  13.8 11.0 %copy-start.5 = (f32[2,384]{1,0:T(2,128)S(1)}, f32[2,384]{1,0:T(2,128)}, u32[]{:S(2)}) copy-start(f32[2,384]{1,0:T(2,128)} %refs_11_.11) | copy-start | bytes 9220
  25.8 2.0 %collective-permute-start.4 = (bf16[2,192,384]{2,1,0:T(8,128)(2,1)S(1)}, bf16[2,192,384]{2,1,0:T(8,128)(2,1)S(1)}, u32[]{:S(2)}, u32[]{:S(2)}) collective-permute-start(bf16[2,192,384]{2,1,0:T(8,128)(2,1)S(1)} %get-tuple-element.172), channel_id=1, source_target_pairs={{0,2},{2,0},{4,6},{6,4},{8,10},{10,8},{12,14},{14,12},{16,18},{18,... | collective-permute-start | bytes 884744 | tf_op jit(solution)/shard_map/ppermute | solution.py:876
  27.8 6.3 %collective-permute-start.5 = (bf16[192,384]{1,0:T(8,128)(2,1)S(1)}, bf16[192,384]{1,0:T(8,128)(2,1)S(1)}, u32[]{:S(2)}, u32[]{:S(2)}) collective-permute-start(bf16[192,384]{1,0:T(8,128)(2,1)S(1)} %get-tuple-element.175), channel_id=1, source_target_pairs={{0,4},{2,6},{4,0},{6,2},{8,12},{10,14},{12,8},{14,10},{16,20},{18,... | collective-permute-start | bytes 442376 | tf_op jit(solution)/shard_map/ppermute | solution.py:876
  34.2 5.8 %collective-permute-start.6 = (bf16[192,384]{1,0:T(8,128)(2,1)S(1)}, bf16[192,384]{1,0:T(8,128)(2,1)S(1)}, u32[]{:S(2)}, u32[]{:S(2)}) collective-permute-start(bf16[192,384]{1,0:T(8,128)(2,1)S(1)} %get-tuple-element.182), channel_id=1, source_target_pairs={{0,8},{2,10},{4,12},{6,14},{8,0},{10,2},{12,4},{14,6},{16,24},{18,... | collective-permute-start | bytes 442376 | tf_op jit(solution)/shard_map/ppermute | solution.py:876
  40.0 10.8 %collective-permute-start.8 = (bf16[192,384]{1,0:T(8,128)(2,1)S(1)}, bf16[192,384]{1,0:T(8,128)(2,1)S(1)}, u32[]{:S(2)}, u32[]{:S(2)}) collective-permute-start(bf16[192,384]{1,0:T(8,128)(2,1)S(1)} %get-tuple-element.194), channel_id=1, source_target_pairs={{0,16},{2,18},{4,20},{6,22},{8,24},{10,26},{12,28},{14,30},{16,0},... | collective-permute-start | bytes 442376 | tf_op jit(solution)/shard_map/ppermute | solution.py:876
  42.6 4.5 %collective-permute-start.3 = (bf16[256,128]{1,0:T(8,128)(2,1)S(1)}, bf16[256,128]{1,0:T(8,128)(2,1)S(1)}, u32[]{:S(2)}, u32[]{:S(2)}) collective-permute-start(bf16[256,128]{1,0:T(8,128)(2,1)S(1)} %get-tuple-element.159), channel_id=1, source_target_pairs={{1,0},{0,1},{3,2},{2,3},{5,4},{4,5},{7,6},{6,7},{9,8},{8,9},{11,10... | collective-permute-start | bytes 196616 | tf_op jit(solution)/shard_map/ppermute | solution.py:861
  46.4 4.3 %collective-permute-start.7 = (bf16[256,128]{1,0:T(8,128)(2,1)S(1)}, bf16[256,128]{1,0:T(8,128)(2,1)S(1)}, u32[]{:S(2)}, u32[]{:S(2)}) collective-permute-start(bf16[256,128]{1,0:T(8,128)(2,1)S(1)} %get-tuple-element.189), channel_id=1, source_target_pairs={{1,0},{0,1},{3,2},{2,3},{5,4},{4,5},{7,6},{6,7},{9,8},{8,9},{11,10... | collective-permute-start | bytes 196616 | tf_op jit(solution)/shard_map/ppermute | solution.py:861
  52.3 1.6 %collective-permute-start.10 = (bf16[2,160,384]{2,1,0:T(8,128)(2,1)S(1)}, bf16[2,160,384]{2,1,0:T(8,128)(2,1)S(1)}, u32[]{:S(2)}, u32[]{:S(2)}) collective-permute-start(bf16[2,160,384]{2,1,0:T(8,128)(2,1)S(1)} %get-tuple-element.220), channel_id=1, source_target_pairs={{0,2},{2,0},{4,6},{6,4},{8,10},{10,8},{12,14},{14,12},{16,18},{18,... | collective-permute-start | bytes 737288 | tf_op jit(solution)/shard_map/ppermute | solution.py:876
  53.2 8.9 %collective-permute-start.9 = (bf16[352,384]{1,0:T(8,128)(2,1)S(1)}, bf16[352,384]{1,0:T(8,128)(2,1)S(1)}, u32[]{:S(2)}, u32[]{:S(2)}) collective-permute-start(bf16[352,384]{1,0:T(8,128)(2,1)S(1)} %stack_kernel.3), channel_id=1, source_target_pairs={{0,1},{1,0},{2,3},{3,2},{4,5},{5,4},{6,7},{7,6},{8,9},{9,8},{10,11... | collective-permute-start | bytes 811016 | tf_op jit(solution)/shard_map/ppermute | solution.py:867
  54.0 5.5 %collective-permute-start.11 = (bf16[160,384]{1,0:T(8,128)(2,1)S(1)}, bf16[160,384]{1,0:T(8,128)(2,1)S(1)}, u32[]{:S(2)}, u32[]{:S(2)}) collective-permute-start(bf16[160,384]{1,0:T(8,128)(2,1)S(1)} %get-tuple-element.222), channel_id=1, source_target_pairs={{0,4},{2,6},{4,0},{6,2},{8,12},{10,14},{12,8},{14,10},{16,20},{18,... | collective-permute-start | bytes 368648 | tf_op jit(solution)/shard_map/ppermute | solution.py:876
  59.5 5.1 %collective-permute-start.12 = (bf16[160,384]{1,0:T(8,128)(2,1)S(1)}, bf16[160,384]{1,0:T(8,128)(2,1)S(1)}, u32[]{:S(2)}, u32[]{:S(2)}) collective-permute-start(bf16[160,384]{1,0:T(8,128)(2,1)S(1)} %get-tuple-element.224), channel_id=1, source_target_pairs={{0,8},{2,10},{4,12},{6,14},{8,0},{10,2},{12,4},{14,6},{16,24},{18,... | collective-permute-start | bytes 368648 | tf_op jit(solution)/shard_map/ppermute | solution.py:876
  63.1 9.9 %collective-permute-start.15 = (bf16[288,384]{1,0:T(8,128)(2,1)S(1)}, bf16[288,384]{1,0:T(8,128)(2,1)S(1)}, u32[]{:S(2)}, u32[]{:S(2)}) collective-permute-start(bf16[288,384]{1,0:T(8,128)(2,1)S(1)} %stack_kernel.4.refs_0_), channel_id=1, source_target_pairs={{0,4},{2,6},{4,0},{6,2},{8,12},{10,14},{12,8},{14,10},{16,20},{18,... | collective-permute-start | bytes 663560 | tf_op jit(solution)/shard_map/ppermute | solution.py:876
  64.7 8.3 %collective-permute-start.13 = (bf16[160,384]{1,0:T(8,128)(2,1)S(1)}, bf16[160,384]{1,0:T(8,128)(2,1)S(1)}, u32[]{:S(2)}, u32[]{:S(2)}) collective-permute-start(bf16[160,384]{1,0:T(8,128)(2,1)S(1)} %get-tuple-element.227), channel_id=1, source_target_pairs={{0,16},{2,18},{4,20},{6,22},{8,24},{10,26},{12,28},{14,30},{16,0},... | collective-permute-start | bytes 368648 | tf_op jit(solution)/shard_map/ppermute | solution.py:876
  73.0 3.7 %collective-permute-start.16 = (bf16[2,288,384]{2,1,0:T(8,128)(2,1)S(1)}, bf16[2,288,384]{2,1,0:T(8,128)(2,1)S(1)}, u32[]{:S(2)}, u32[]{:S(2)}) collective-permute-start(bf16[2,288,384]{2,1,0:T(8,128)(2,1)S(1)} %bitcast.3), channel_id=1, source_target_pairs={{0,2},{2,0},{4,6},{6,4},{8,10},{10,8},{12,14},{14,12},{16,18},{18,... | collective-permute-start | bytes 1327112 | tf_op jit(solution)/shard_map/ppermute | solution.py:876
  73.1 7.7 %collective-permute-start.18 = (bf16[112,384]{1,0:T(8,128)(2,1)S(1)}, bf16[112,384]{1,0:T(8,128)(2,1)S(1)}, u32[]{:S(2)}, u32[]{:S(2)}) collective-permute-start(bf16[112,384]{1,0:T(8,128)(2,1)S(1)} %slice.4), channel_id=1, source_target_pairs={{5,0},{4,1},{7,2},{6,3},{1,4},{0,5},{3,6},{2,7},{13,8},{12,9},{15,... | collective-permute-start | bytes 258056 | tf_op jit(solution)/shard_map/ppermute | solution.py:1148
  74.2 6.5 %collective-permute-start.14 = (bf16[112,384]{1,0:T(8,128)(2,1)S(1)}, bf16[112,384]{1,0:T(8,128)(2,1)S(1)}, u32[]{:S(2)}, u32[]{:S(2)}) collective-permute-start(bf16[112,384]{1,0:T(8,128)(2,1)S(1)} %slice.4), channel_id=1, source_target_pairs={{1,0},{0,1},{3,2},{2,3},{5,4},{4,5},{7,6},{6,7},{9,8},{8,9},{11,10... | collective-permute-start | bytes 258056 | tf_op jit(solution)/shard_map/ppermute | solution.py:1148
  75.2 5.6 %collective-permute-start.17 = (bf16[160,384]{1,0:T(8,128)(2,1)S(1)}, bf16[160,384]{1,0:T(8,128)(2,1)S(1)}, u32[]{:S(2)}, u32[]{:S(2)}) collective-permute-start(bf16[160,384]{1,0:T(8,128)(2,1)S(1)} %add_kernel.15.refs_2_.base_ref), channel_id=1, source_target_pairs={{4,0},{5,1},{6,2},{7,3},{0,4},{1,5},{2,6},{3,7},{12,8},{13,9},{14,... | collective-permute-start | bytes 368648 | tf_op jit(solution)/shard_map/ppermute | solution.py:1148
  80.8 1.5 %collective-permute-start.19 = (bf16[256,384]{1,0:T(8,128)(2,1)S(1)}, bf16[256,384]{1,0:T(8,128)(2,1)S(1)}, u32[]{:S(2)}, u32[]{:S(2)}) collective-permute-start(bf16[256,384]{1,0:T(8,128)(2,1)S(1)} %join_kernel.2.refs_0_), channel_id=1, source_target_pairs={{0,2},{2,0},{4,6},{6,4},{8,10},{10,8},{12,14},{14,12},{16,18},{18,... | collective-permute-start | bytes 589832 | tf_op jit(solution)/shard_map/ppermute | solution.py:876
  80.9 1.7 %collective-permute-start.20 = (bf16[256,384]{1,0:T(8,128)(2,1)S(1)}, bf16[256,384]{1,0:T(8,128)(2,1)S(1)}, u32[]{:S(2)}, u32[]{:S(2)}) collective-permute-start(bf16[256,384]{1,0:T(8,128)(2,1)S(1)} %join_kernel.3.refs_1_), channel_id=1, source_target_pairs={{0,2},{2,0},{4,6},{6,4},{8,10},{10,8},{12,14},{14,12},{16,18},{18,... | collective-permute-start | bytes 589832 | tf_op jit(solution)/shard_map/ppermute | solution.py:876
  (3 other events, 22.0 us)

commit v3 on v2

--- a/solution.py
+++ b/solution.py
@@ -16,7 +16,7 @@
 HUGE_STEP = 1e30
 LOG2E = math.log2(math.e)
 LN2 = math.log(2.0)
-BLOCK = 128
+BLOCK = 256
 PAIRS = 8
 PIECES = 4
 

time: 84.2 us -> 82.6 us (0.981)
  Pallas kernels: 39.4 us -> 37.2 us
    pallas_call x35, Pallas kernels: 39.4 us -> 37.2 us  [kernel_call(): pl.pallas_call(kernel, name=name, out_shape=outs, in_specs=specs, out_spe...]
  transfers between devices with their start and end apart: 21 -> 21, of which waited for: 9 -> 9; matrix products, arithmetic and copies ran while one was open for 0% -> 0% of each run, Pallas kernels for 28% -> 27%
where the time goes in v3:
time: 82.6 us; the launch traced here: 82.4 us
  Pallas kernels  37.2 us (45%)
  starting transfers between devices  23.6 us (29%)
  waiting for transfers between devices  20.2 us (24%)
  between operations  1.2 us (1%)
    pallas_call x35, Pallas kernels, kernel_call(): pl.pallas_call(kernel, name=name, out_shape=outs, in_specs=specs, out_spe...  37.2 us
    ppermute x12, waiting for transfers between devices, swap(): return lax.ppermute(x, 'tok', partner_pairs(n_tok, stride))  13.2 us
    ppermute x12, starting transfers between devices, swap(): return lax.ppermute(x, 'tok', partner_pairs(n_tok, stride))  12.1 us
    ppermute x5, starting transfers between devices, rotated(): lax.ppermute(x, 'ch', [((i + k) % n_ch, i) for i in range(n_ch)])  7.28 us
    ppermute x3, starting transfers between devices, local(): lax.ppermute(shared if c else late.own, ('tok', 'ch'), pairs)  3.55 us
    ppermute x5, waiting for transfers between devices, rotated(): lax.ppermute(x, 'ch', [((i + k) % n_ch, i) for i in range(n_ch)])  3.29 us
    ppermute x3, waiting for transfers between devices, local(): lax.ppermute(shared if c else late.own, ('tok', 'ch'), pairs)  2.65 us
  transfers between devices with their start and end apart: 21, of which 9 were waited for; matrix products, arithmetic and copies ran while one was open for 0% of the time, Pallas kernels for 27%

profile of v3, /device:TPU:0, one launch (start us, length us, event | category | flops | bytes accessed | tf_op | source)
XLA Modules:
  0.0 82.4 jit_solution(4892855254529111762)
XLA Ops:
  0.6 3.0 %collective-permute-start.1 = (bf16[128,384]{1,0:T(8,128)(2,1)}, bf16[128,384]{1,0:T(8,128)(2,1)S(1)}, u32[]{:S(2)}, u32[]{:S(2)}) collective-permute-start(bf16[128,384]{1,0:T(8,128)(2,1)} %own_hbm.1), channel_id=1, source_target_pairs={{1,0},{0,1},{3,2},{2,3},{5,4},{4,5},{7,6},{6,7},{9,8},{8,9},{11,10... | collective-permute-start | bytes 294920 | tf_op jit(solution)/shard_map/ppermute | solution.py:861
  6.0 2.1 %collective-permute-start = (bf16[128,384]{1,0:T(8,128)(2,1)S(1)}, bf16[128,384]{1,0:T(8,128)(2,1)S(1)}, u32[]{:S(2)}, u32[]{:S(2)}) collective-permute-start(bf16[128,384]{1,0:T(8,128)(2,1)S(1)} %get-tuple-element.127.refs_0_.cot_ref), channel_id=1, source_target_pairs={{1,0},{0,1},{3,2},{2,3},{5,4},{4,5},{7,6},{6,7},{9,8},{8,9},{11,10... | collective-permute-start | bytes 294920 | tf_op jit(solution)/shard_map/ppermute | solution.py:861
  10.6 1.7 %front_kernel.1 = (f32[2,256,128]{2,1,0:T(8,128)S(1)}, f32[3,256,128]{2,1,0:T(8,128)S(1)}, f32[3,256,128]{2,1,0:T(8,128)S(1)}, f32[3,256,128]{2,1,0:T(8,128)S(1)}, f32[3,256,128]{2,1,0:T(8,128)S(1)}) custom-call(bf16[160,384]{1,0:T(8,128)(2,1)S(1)} %collective-permute-done.2.refs_0_, bf16[2,256,384]{2,1,0:T(8,128)(2,1)S(1)} %get-tuple-element.131.sigs_ref.refs_1_.refs_7_, ...), custom_call_target="tpu_custom_call" | custom-call | flops 10000000 | bytes 30000 | tf_op jit(solution)/shard_map/front_kernel/pallas_call | solution.py:846
  13.0 5.6 %forward_kernel_1.1 = (f32[3,256,128]{2,1,0:T(8,128)S(1)}, f32[3,16,8,128]{3,2,1,0:T(8,128)S(1)}, f32[256,2048]{1,0:T(8,128)S(1)}, f32[256,2048]{1,0:T(8,128)S(1...) custom-call(f32[3,256,128]{2,1,0:T(8,128)S(1)} %get-tuple-element.136.gy_ref.refs_0_, ...), custom_call_target="tpu_custom_call" | custom-call | flops 10000000 | bytes 30000 | tf_op jit(solution)/shard_map/forward_kernel_1/pallas_call | solution.py:846
  18.6 5.4 %forward_kernel_0.1 = (f32[3,256,128]{2,1,0:T(8,128)S(1)}, f32[3,16,8,128]{3,2,1,0:T(8,128)S(1)}, f32[256,2048]{1,0:T(8,128)S(1)}, f32[256,2048]{1,0:T(8,128)S(1...) custom-call(f32[3,256,128]{2,1,0:T(8,128)S(1)} %get-tuple-element.136.gy_ref.refs_0_, ...), custom_call_target="tpu_custom_call" | custom-call | flops 10000000 | bytes 30000 | tf_op jit(solution)/shard_map/forward_kernel_0/pallas_call | solution.py:846
  25.0 1.8 %backward_kernel_00.1 = (f32[256,128]{1,0:T(8,128)S(1)}, bf16[256,2048]{1,0:T(8,128)(2,1)S(1)}, f32[256,128]{1,0:T(8,128)S(1)}, f32[24,128]{1,0:T(8,128)S(1)}, f...) custom-call(f32[3,256,128]{2,1,0:T(8,128)S(1)} %get-tuple-element.136.gy_ref.refs_0_, ...), custom_call_target="tpu_custom_call" | custom-call | flops 5000000 | bytes 15000 | tf_op jit(solution)/shard_map/backward_kernel_00/pallas_call | solution.py:846
  26.9 1.6 %collective-permute-start.5 = (bf16[192,384]{1,0:T(8,128)(2,1)S(1)}, bf16[192,384]{1,0:T(8,128)(2,1)S(1)}, u32[]{:S(2)}, u32[]{:S(2)}) collective-permute-start(bf16[192,384]{1,0:T(8,128)(2,1)S(1)} %get-tuple-element.175), channel_id=1, source_target_pairs={{0,4},{2,6},{4,0},{6,2},{8,12},{10,14},{12,8},{14,10},{16,20},{18,... | collective-permute-start | bytes 442376 | tf_op jit(solution)/shard_map/ppermute | solution.py:876
  28.5 1.9 %backward_kernel_01.1 = (f32[256,128]{1,0:T(8,128)S(1)}, bf16[256,2048]{1,0:T(8,128)(2,1)S(1)}, f32[256,128]{1,0:T(8,128)S(1)}, f32[24,128]{1,0:T(8,128)S(1)}, f...) custom-call(f32[3,256,128]{2,1,0:T(8,128)S(1)} %get-tuple-element.136.gy_ref.refs_0_, ...), custom_call_target="tpu_custom_call" | custom-call | flops 5000000 | bytes 15000 | tf_op jit(solution)/shard_map/backward_kernel_01/pallas_call | solution.py:846
  30.4 2.3 %backward_kernel_02.1 = (f32[256,128]{1,0:T(8,128)S(1)}, bf16[256,128]{1,0:T(8,128)(2,1)S(1)}, f32[256,128]{1,0:T(8,128)S(1)}, f32[24,128]{1,0:T(8,128)S(1)}, f3...) custom-call(f32[3,256,128]{2,1,0:T(8,128)S(1)} %get-tuple-element.136.gy_ref.refs_0_, ...), custom_call_target="tpu_custom_call" | custom-call | flops 5000000 | bytes 15000 | tf_op jit(solution)/shard_map/backward_kernel_02/pallas_call | solution.py:846
  33.2 1.7 %collective-permute-start.6 = (bf16[192,384]{1,0:T(8,128)(2,1)S(1)}, bf16[192,384]{1,0:T(8,128)(2,1)S(1)}, u32[]{:S(2)}, u32[]{:S(2)}) collective-permute-start(bf16[192,384]{1,0:T(8,128)(2,1)S(1)} %get-tuple-element.182), channel_id=1, source_target_pairs={{0,8},{2,10},{4,12},{6,14},{8,0},{10,2},{12,4},{14,6},{16,24},{18,... | collective-permute-start | bytes 442376 | tf_op jit(solution)/shard_map/ppermute | solution.py:876
  34.9 1.9 %backward_kernel_10.1 = (f32[256,128]{1,0:T(8,128)S(1)}, bf16[256,2048]{1,0:T(8,128)(2,1)S(1)}, f32[256,128]{1,0:T(8,128)S(1)}, f32[24,128]{1,0:T(8,128)S(1)}, f...) custom-call(f32[3,256,128]{2,1,0:T(8,128)S(1)} %get-tuple-element.136.gy_ref.refs_0_, ...), custom_call_target="tpu_custom_call" | custom-call | flops 5000000 | bytes 15000 | tf_op jit(solution)/shard_map/backward_kernel_10/pallas_call | solution.py:846
  36.8 2.1 %backward_kernel_11.1 = (f32[256,128]{1,0:T(8,128)S(1)}, bf16[256,2048]{1,0:T(8,128)(2,1)S(1)}, f32[256,128]{1,0:T(8,128)S(1)}, f32[24,128]{1,0:T(8,128)S(1)}, f...) custom-call(f32[3,256,128]{2,1,0:T(8,128)S(1)} %get-tuple-element.136.gy_ref.refs_0_, ...), custom_call_target="tpu_custom_call" | custom-call | flops 5000000 | bytes 15000 | tf_op jit(solution)/shard_map/backward_kernel_11/pallas_call | solution.py:846
  38.9 2.6 %collective-permute-start.8 = (bf16[192,384]{1,0:T(8,128)(2,1)S(1)}, bf16[192,384]{1,0:T(8,128)(2,1)S(1)}, u32[]{:S(2)}, u32[]{:S(2)}) collective-permute-start(bf16[192,384]{1,0:T(8,128)(2,1)S(1)} %get-tuple-element.194), channel_id=1, source_target_pairs={{0,16},{2,18},{4,20},{6,22},{8,24},{10,26},{12,28},{14,30},{16,0},... | collective-permute-start | bytes 442376 | tf_op jit(solution)/shard_map/ppermute | solution.py:876
  41.6 1.4 %collective-permute-start.3 = (bf16[256,128]{1,0:T(8,128)(2,1)S(1)}, bf16[256,128]{1,0:T(8,128)(2,1)S(1)}, u32[]{:S(2)}, u32[]{:S(2)}) collective-permute-start(bf16[256,128]{1,0:T(8,128)(2,1)S(1)} %get-tuple-element.159), channel_id=1, source_target_pairs={{1,0},{0,1},{3,2},{2,3},{5,4},{4,5},{7,6},{6,7},{9,8},{8,9},{11,10... | collective-permute-start | bytes 196616 | tf_op jit(solution)/shard_map/ppermute | solution.py:861
  43.0 2.3 %backward_kernel_12.1 = (f32[256,128]{1,0:T(8,128)S(1)}, bf16[256,128]{1,0:T(8,128)(2,1)S(1)}, f32[256,128]{1,0:T(8,128)S(1)}, f32[24,128]{1,0:T(8,128)S(1)}, f3...) custom-call(f32[3,256,128]{2,1,0:T(8,128)S(1)} %get-tuple-element.136.gy_ref.refs_0_, ...), custom_call_target="tpu_custom_call" | custom-call | flops 5000000 | bytes 15000 | tf_op jit(solution)/shard_map/backward_kernel_12/pallas_call | solution.py:846
  47.2 2.5 %collective-permute-done.7.refs_1_ = bf16[256,128]{1,0:T(8,128)(2,1)S(1)} collective-permute-done((bf16[256,128]{1,0:T(8,128)(2,1)S(1)}, bf16[256,128]{1,0:T(8,128)(2,1)S(1)}, u32[]{:S(2)}, u32[]{:S(2)}) %collective-permute-start.7) | collective-permute-done | bytes 65568 | tf_op jit(solution)/shard_map/ppermute | solution.py:861
  52.3 1.6 %collective-permute-start.11 = (bf16[160,384]{1,0:T(8,128)(2,1)S(1)}, bf16[160,384]{1,0:T(8,128)(2,1)S(1)}, u32[]{:S(2)}, u32[]{:S(2)}) collective-permute-start(bf16[160,384]{1,0:T(8,128)(2,1)S(1)} %get-tuple-element.222), channel_id=1, source_target_pairs={{0,4},{2,6},{4,0},{6,2},{8,12},{10,14},{12,8},{14,10},{16,20},{18,... | collective-permute-start | bytes 368648 | tf_op jit(solution)/shard_map/ppermute | solution.py:876
  53.9 3.9 %collective-permute-done.11.got_ref = bf16[160,384]{1,0:T(8,128)(2,1)S(1)} collective-permute-done((bf16[160,384]{1,0:T(8,128)(2,1)S(1)}, bf16[160,384]{1,0:T(8,128)(2,1)S(1)}, u32[]{:S(2)}, u32[]{:S(2)}) %collective-permute-start.11) | collective-permute-done | bytes 122912 | tf_op jit(solution)/shard_map/ppermute | solution.py:876
  57.9 1.6 %collective-permute-start.12 = (bf16[160,384]{1,0:T(8,128)(2,1)S(1)}, bf16[160,384]{1,0:T(8,128)(2,1)S(1)}, u32[]{:S(2)}, u32[]{:S(2)}) collective-permute-start(bf16[160,384]{1,0:T(8,128)(2,1)S(1)} %get-tuple-element.224), channel_id=1, source_target_pairs={{0,8},{2,10},{4,12},{6,14},{8,0},{10,2},{12,4},{14,6},{16,24},{18,... | collective-permute-start | bytes 368648 | tf_op jit(solution)/shard_map/ppermute | solution.py:876
  61.4 1.6 %collective-permute-start.15 = (bf16[288,384]{1,0:T(8,128)(2,1)S(1)}, bf16[288,384]{1,0:T(8,128)(2,1)S(1)}, u32[]{:S(2)}, u32[]{:S(2)}) collective-permute-start(bf16[288,384]{1,0:T(8,128)(2,1)S(1)} %stack_kernel.4.refs_0_), channel_id=1, source_target_pairs={{0,4},{2,6},{4,0},{6,2},{8,12},{10,14},{12,8},{14,10},{16,20},{18,... | collective-permute-start | bytes 663560 | tf_op jit(solution)/shard_map/ppermute | solution.py:876
  63.7 7.6 %collective-permute-done.13.got_ref = bf16[160,384]{1,0:T(8,128)(2,1)S(1)} collective-permute-done((bf16[160,384]{1,0:T(8,128)(2,1)S(1)}, bf16[160,384]{1,0:T(8,128)(2,1)S(1)}, u32[]{:S(2)}, u32[]{:S(2)}) %collective-permute-start.13) | collective-permute-done | bytes 122912 | tf_op jit(solution)/shard_map/ppermute | solution.py:876
  73.5 1.5 %collective-permute-start.17 = (bf16[160,384]{1,0:T(8,128)(2,1)S(1)}, bf16[160,384]{1,0:T(8,128)(2,1)S(1)}, u32[]{:S(2)}, u32[]{:S(2)}) collective-permute-start(bf16[160,384]{1,0:T(8,128)(2,1)S(1)} %add_kernel.15.refs_2_.base_ref), channel_id=1, source_target_pairs={{4,0},{5,1},{6,2},{7,3},{0,4},{1,5},{2,6},{3,7},{12,8},{13,9},{14,... | collective-permute-start | bytes 368648 | tf_op jit(solution)/shard_map/ppermute | solution.py:1148
  76.4 2.6 %collective-permute-done.14.refs_0_ = bf16[112,384]{1,0:T(8,128)(2,1)S(1)} collective-permute-done((bf16[112,384]{1,0:T(8,128)(2,1)S(1)}, bf16[112,384]{1,0:T(8,128)(2,1)S(1)}, u32[]{:S(2)}, u32[]{:S(2)}) %collective-permute-start.14) | collective-permute-done | bytes 86048 | tf_op jit(solution)/shard_map/ppermute | solution.py:1148
  80.9 1.3 %late_result_kernel.1 = (f32[384,1536]{1,0:T(8,128)}, f32[384]{0:T(512)}, f32[2,4,384]{2,1,0:T(4,128)}, f32[2,384]{1,0:T(2,128)}, f32[2,56,384]{2,1,0:T(8,128)},...) custom-call(bf16[256,384]{1,0:T(8,128)(2,1)S(1)} %join_kernel.2.refs, ...), custom_call_target="tpu_custom_call", output_to_operand_aliasing={{0}: (4, {})} | custom-call | flops 20000000 | bytes 60000 | tf_op jit(solution)/shard_map/late_result_kernel/pallas_call | solution.py:846
  (67 shorter events, 19.6 us)
Async XLA Ops:
  0.6 7.5 %collective-permute-start.1 = (bf16[128,384]{1,0:T(8,128)(2,1)}, bf16[128,384]{1,0:T(8,128)(2,1)S(1)}, u32[]{:S(2)}, u32[]{:S(2)}) collective-permute-start(bf16[128,384]{1,0:T(8,128)(2,1)} %own_hbm.1), channel_id=1, source_target_pairs={{1,0},{0,1},{3,2},{2,3},{5,4},{4,5},{7,6},{6,7},{9,8},{8,9},{11,10... | collective-permute-start | bytes 294920 | tf_op jit(solution)/shard_map/ppermute | solution.py:861
  4.7 7.7 %copy-start.4 = (bf16[384,384]{1,0:T(8,128)(2,1)S(1)}, bf16[384,384]{1,0:T(8,128)(2,1)}, u32[]{:S(2)}) copy-start(bf16[384,384]{1,0:T(8,128)(2,1)} %wout_ref.1) | copy-start | bytes 884740
  4.7 6.0 %collective-permute-start.2 = (bf16[160,384]{1,0:T(8,128)(2,1)S(1)}, bf16[160,384]{1,0:T(8,128)(2,1)S(1)}, u32[]{:S(2)}, u32[]{:S(2)}) collective-permute-start(bf16[160,384]{1,0:T(8,128)(2,1)S(1)} %weight_kernel.1._.pack_ref.refs_8_), channel_id=1, source_target_pairs={{1,0},{0,1},{3,2},{2,3},{5,4},{4,5},{7,6},{6,7},{9,8},{8,9},{11,10... | collective-permute-start | bytes 368648 | tf_op jit(solution)/shard_map/ppermute | solution.py:861
  6.0 6.9 %copy-start = (bf16[2048,128]{1,0:T(8,128)(2,1)S(1)}, bf16[2048,128]{1,0:T(8,128)(2,1)}, u32[]{:S(2)}) copy-start(bf16[2048,128]{1,0:T(8,128)(2,1)} %constant.5.clone.er_ref.refs_13_) | copy-start | bytes 1572868
  6.0 6.3 %collective-permute-start = (bf16[128,384]{1,0:T(8,128)(2,1)S(1)}, bf16[128,384]{1,0:T(8,128)(2,1)S(1)}, u32[]{:S(2)}, u32[]{:S(2)}) collective-permute-start(bf16[128,384]{1,0:T(8,128)(2,1)S(1)} %get-tuple-element.127.refs_0_.cot_ref), channel_id=1, source_target_pairs={{1,0},{0,1},{3,2},{2,3},{5,4},{4,5},{7,6},{6,7},{9,8},{8,9},{11,10... | collective-permute-start | bytes 294920 | tf_op jit(solution)/shard_map/ppermute | solution.py:861
  13.0 11.0 %copy-start.5 = (f32[2,384]{1,0:T(2,128)S(1)}, f32[2,384]{1,0:T(2,128)}, u32[]{:S(2)}) copy-start(f32[2,384]{1,0:T(2,128)} %refs_11_.11) | copy-start | bytes 9220
  24.9 1.9 %collective-permute-start.4 = (bf16[2,192,384]{2,1,0:T(8,128)(2,1)S(1)}, bf16[2,192,384]{2,1,0:T(8,128)(2,1)S(1)}, u32[]{:S(2)}, u32[]{:S(2)}) collective-permute-start(bf16[2,192,384]{2,1,0:T(8,128)(2,1)S(1)} %get-tuple-element.172), channel_id=1, source_target_pairs={{0,2},{2,0},{4,6},{6,4},{8,10},{10,8},{12,14},{14,12},{16,18},{18,... | collective-permute-start | bytes 884744 | tf_op jit(solution)/shard_map/ppermute | solution.py:876
  26.9 6.3 %collective-permute-start.5 = (bf16[192,384]{1,0:T(8,128)(2,1)S(1)}, bf16[192,384]{1,0:T(8,128)(2,1)S(1)}, u32[]{:S(2)}, u32[]{:S(2)}) collective-permute-start(bf16[192,384]{1,0:T(8,128)(2,1)S(1)} %get-tuple-element.175), channel_id=1, source_target_pairs={{0,4},{2,6},{4,0},{6,2},{8,12},{10,14},{12,8},{14,10},{16,20},{18,... | collective-permute-start | bytes 442376 | tf_op jit(solution)/shard_map/ppermute | solution.py:876
  33.2 5.6 %collective-permute-start.6 = (bf16[192,384]{1,0:T(8,128)(2,1)S(1)}, bf16[192,384]{1,0:T(8,128)(2,1)S(1)}, u32[]{:S(2)}, u32[]{:S(2)}) collective-permute-start(bf16[192,384]{1,0:T(8,128)(2,1)S(1)} %get-tuple-element.182), channel_id=1, source_target_pairs={{0,8},{2,10},{4,12},{6,14},{8,0},{10,2},{12,4},{14,6},{16,24},{18,... | collective-permute-start | bytes 442376 | tf_op jit(solution)/shard_map/ppermute | solution.py:876
  38.9 10.7 %collective-permute-start.8 = (bf16[192,384]{1,0:T(8,128)(2,1)S(1)}, bf16[192,384]{1,0:T(8,128)(2,1)S(1)}, u32[]{:S(2)}, u32[]{:S(2)}) collective-permute-start(bf16[192,384]{1,0:T(8,128)(2,1)S(1)} %get-tuple-element.194), channel_id=1, source_target_pairs={{0,16},{2,18},{4,20},{6,22},{8,24},{10,26},{12,28},{14,30},{16,0},... | collective-permute-start | bytes 442376 | tf_op jit(solution)/shard_map/ppermute | solution.py:876
  41.6 4.4 %collective-permute-start.3 = (bf16[256,128]{1,0:T(8,128)(2,1)S(1)}, bf16[256,128]{1,0:T(8,128)(2,1)S(1)}, u32[]{:S(2)}, u32[]{:S(2)}) collective-permute-start(bf16[256,128]{1,0:T(8,128)(2,1)S(1)} %get-tuple-element.159), channel_id=1, source_target_pairs={{1,0},{0,1},{3,2},{2,3},{5,4},{4,5},{7,6},{6,7},{9,8},{8,9},{11,10... | collective-permute-start | bytes 196616 | tf_op jit(solution)/shard_map/ppermute | solution.py:861
  45.3 4.3 %collective-permute-start.7 = (bf16[256,128]{1,0:T(8,128)(2,1)S(1)}, bf16[256,128]{1,0:T(8,128)(2,1)S(1)}, u32[]{:S(2)}, u32[]{:S(2)}) collective-permute-start(bf16[256,128]{1,0:T(8,128)(2,1)S(1)} %get-tuple-element.189), channel_id=1, source_target_pairs={{1,0},{0,1},{3,2},{2,3},{5,4},{4,5},{7,6},{6,7},{9,8},{8,9},{11,10... | collective-permute-start | bytes 196616 | tf_op jit(solution)/shard_map/ppermute | solution.py:861
  50.7 1.6 %collective-permute-start.10 = (bf16[2,160,384]{2,1,0:T(8,128)(2,1)S(1)}, bf16[2,160,384]{2,1,0:T(8,128)(2,1)S(1)}, u32[]{:S(2)}, u32[]{:S(2)}) collective-permute-start(bf16[2,160,384]{2,1,0:T(8,128)(2,1)S(1)} %get-tuple-element.220), channel_id=1, source_target_pairs={{0,2},{2,0},{4,6},{6,4},{8,10},{10,8},{12,14},{14,12},{16,18},{18,... | collective-permute-start | bytes 737288 | tf_op jit(solution)/shard_map/ppermute | solution.py:876
  51.6 8.9 %collective-permute-start.9 = (bf16[352,384]{1,0:T(8,128)(2,1)S(1)}, bf16[352,384]{1,0:T(8,128)(2,1)S(1)}, u32[]{:S(2)}, u32[]{:S(2)}) collective-permute-start(bf16[352,384]{1,0:T(8,128)(2,1)S(1)} %stack_kernel.3), channel_id=1, source_target_pairs={{0,1},{1,0},{2,3},{3,2},{4,5},{5,4},{6,7},{7,6},{8,9},{9,8},{10,11... | collective-permute-start | bytes 811016 | tf_op jit(solution)/shard_map/ppermute | solution.py:867
  52.3 5.5 %collective-permute-start.11 = (bf16[160,384]{1,0:T(8,128)(2,1)S(1)}, bf16[160,384]{1,0:T(8,128)(2,1)S(1)}, u32[]{:S(2)}, u32[]{:S(2)}) collective-permute-start(bf16[160,384]{1,0:T(8,128)(2,1)S(1)} %get-tuple-element.222), channel_id=1, source_target_pairs={{0,4},{2,6},{4,0},{6,2},{8,12},{10,14},{12,8},{14,10},{16,20},{18,... | collective-permute-start | bytes 368648 | tf_op jit(solution)/shard_map/ppermute | solution.py:876
  57.9 5.1 %collective-permute-start.12 = (bf16[160,384]{1,0:T(8,128)(2,1)S(1)}, bf16[160,384]{1,0:T(8,128)(2,1)S(1)}, u32[]{:S(2)}, u32[]{:S(2)}) collective-permute-start(bf16[160,384]{1,0:T(8,128)(2,1)S(1)} %get-tuple-element.224), channel_id=1, source_target_pairs={{0,8},{2,10},{4,12},{6,14},{8,0},{10,2},{12,4},{14,6},{16,24},{18,... | collective-permute-start | bytes 368648 | tf_op jit(solution)/shard_map/ppermute | solution.py:876
  61.4 9.9 %collective-permute-start.15 = (bf16[288,384]{1,0:T(8,128)(2,1)S(1)}, bf16[288,384]{1,0:T(8,128)(2,1)S(1)}, u32[]{:S(2)}, u32[]{:S(2)}) collective-permute-start(bf16[288,384]{1,0:T(8,128)(2,1)S(1)} %stack_kernel.4.refs_0_), channel_id=1, source_target_pairs={{0,4},{2,6},{4,0},{6,2},{8,12},{10,14},{12,8},{14,10},{16,20},{18,... | collective-permute-start | bytes 663560 | tf_op jit(solution)/shard_map/ppermute | solution.py:876
  63.0 8.3 %collective-permute-start.13 = (bf16[160,384]{1,0:T(8,128)(2,1)S(1)}, bf16[160,384]{1,0:T(8,128)(2,1)S(1)}, u32[]{:S(2)}, u32[]{:S(2)}) collective-permute-start(bf16[160,384]{1,0:T(8,128)(2,1)S(1)} %get-tuple-element.227), channel_id=1, source_target_pairs={{0,16},{2,18},{4,20},{6,22},{8,24},{10,26},{12,28},{14,30},{16,0},... | collective-permute-start | bytes 368648 | tf_op jit(solution)/shard_map/ppermute | solution.py:876
  71.4 3.7 %collective-permute-start.16 = (bf16[2,288,384]{2,1,0:T(8,128)(2,1)S(1)}, bf16[2,288,384]{2,1,0:T(8,128)(2,1)S(1)}, u32[]{:S(2)}, u32[]{:S(2)}) collective-permute-start(bf16[2,288,384]{2,1,0:T(8,128)(2,1)S(1)} %bitcast.3), channel_id=1, source_target_pairs={{0,2},{2,0},{4,6},{6,4},{8,10},{10,8},{12,14},{14,12},{16,18},{18,... | collective-permute-start | bytes 1327112 | tf_op jit(solution)/shard_map/ppermute | solution.py:876
  71.5 7.7 %collective-permute-start.18 = (bf16[112,384]{1,0:T(8,128)(2,1)S(1)}, bf16[112,384]{1,0:T(8,128)(2,1)S(1)}, u32[]{:S(2)}, u32[]{:S(2)}) collective-permute-start(bf16[112,384]{1,0:T(8,128)(2,1)S(1)} %slice.4), channel_id=1, source_target_pairs={{5,0},{4,1},{7,2},{6,3},{1,4},{0,5},{3,6},{2,7},{13,8},{12,9},{15,... | collective-permute-start | bytes 258056 | tf_op jit(solution)/shard_map/ppermute | solution.py:1148
  72.6 6.5 %collective-permute-start.14 = (bf16[112,384]{1,0:T(8,128)(2,1)S(1)}, bf16[112,384]{1,0:T(8,128)(2,1)S(1)}, u32[]{:S(2)}, u32[]{:S(2)}) collective-permute-start(bf16[112,384]{1,0:T(8,128)(2,1)S(1)} %slice.4), channel_id=1, source_target_pairs={{1,0},{0,1},{3,2},{2,3},{5,4},{4,5},{7,6},{6,7},{9,8},{8,9},{11,10... | collective-permute-start | bytes 258056 | tf_op jit(solution)/shard_map/ppermute | solution.py:1148
  73.5 5.6 %collective-permute-start.17 = (bf16[160,384]{1,0:T(8,128)(2,1)S(1)}, bf16[160,384]{1,0:T(8,128)(2,1)S(1)}, u32[]{:S(2)}, u32[]{:S(2)}) collective-permute-start(bf16[160,384]{1,0:T(8,128)(2,1)S(1)} %add_kernel.15.refs_2_.base_ref), channel_id=1, source_target_pairs={{4,0},{5,1},{6,2},{7,3},{0,4},{1,5},{2,6},{3,7},{12,8},{13,9},{14,... | collective-permute-start | bytes 368648 | tf_op jit(solution)/shard_map/ppermute | solution.py:1148
  79.1 1.5 %collective-permute-start.19 = (bf16[256,384]{1,0:T(8,128)(2,1)S(1)}, bf16[256,384]{1,0:T(8,128)(2,1)S(1)}, u32[]{:S(2)}, u32[]{:S(2)}) collective-permute-start(bf16[256,384]{1,0:T(8,128)(2,1)S(1)} %join_kernel.2.refs_0_), channel_id=1, source_target_pairs={{0,2},{2,0},{4,6},{6,4},{8,10},{10,8},{12,14},{14,12},{16,18},{18,... | collective-permute-start | bytes 589832 | tf_op jit(solution)/shard_map/ppermute | solution.py:876
  79.2 1.7 %collective-permute-start.20 = (bf16[256,384]{1,0:T(8,128)(2,1)S(1)}, bf16[256,384]{1,0:T(8,128)(2,1)S(1)}, u32[]{:S(2)}, u32[]{:S(2)}) collective-permute-start(bf16[256,384]{1,0:T(8,128)(2,1)S(1)} %join_kernel.3.refs_1_), channel_id=1, source_target_pairs={{0,2},{2,0},{4,6},{6,4},{8,10},{10,8},{12,14},{14,12},{16,18},{18,... | collective-permute-start | bytes 589832 | tf_op jit(solution)/shard_map/ppermute | solution.py:876
  (3 other events, 20.3 us)
